TPU v7x, 32 devices: a whole 2x2x4 slice. The times are simulated.
32 devices in a mesh: wide: 16 (over z, y, core), narrow: 2 (over x).
Axes of the slice: x: 2, y: 2, z: 4, core: 2. Of those that a mesh axis runs over, the one named last changes fastest.
Arguments:
- hidden_in: bfloat16 [16384, 768], P('wide'), may hold values from -6 to 6
- image_tokens: bfloat16 [128, 256, 768], P('wide', 'narrow'), may hold values from -6 to 6
- image_group: int32 [256], P('wide'), may hold values from 0 to 127, as said below
- caption_len: int32 [256], P('wide'), may hold values from 16 to 64, as said below
- norm_gain: bfloat16 [3, 768], replicated, may hold values from 0.25 to 1.75
- norm_bias: bfloat16 [3, 768], replicated, may hold values from -1 to 1
- self_qkv: bfloat16 [768, 2304], replicated, may hold values from -0.3125 to 0.3125
- self_out: bfloat16 [768, 768], replicated, may hold values from -0.4375 to 0.4375
- cross_query: bfloat16 [768, 768], replicated, may hold values from -0.3125 to 0.3125
- cross_kv: bfloat16 [768, 1536], replicated, may hold values from -0.3125 to 0.3125
- cross_out: bfloat16 [768, 768], replicated, may hold values from -0.875 to 0.875
- mlp_in: bfloat16 [768, 3072], replicated, may hold values from -0.21875 to 0.21875
- mlp_bias_in: bfloat16 [3072], replicated, may hold values from -3 to 3
- mlp_out: bfloat16 [3072, 768], replicated, may hold values from -0.109375 to 0.109375
- mlp_bias_out: bfloat16 [768], replicated, may hold values from -2 to 2
- out_grad: bfloat16 [16384, 768], P('wide'), may hold values from -6 to 6
Outputs:
- hidden_out: bfloat16 [16384, 768], P(('wide', 'narrow'))
- grad_hidden: float32 [16384, 768], P(('wide', 'narrow'))
- grad_image: float32 [128, 256, 768], P('wide', 'narrow')
- grad_norm_gain: float32 [3, 768], P(None, 'narrow')
- grad_norm_bias: float32 [3, 768], P(None, 'narrow')
- grad_self_qkv: float32 [768, 2304], P('narrow')
- grad_self_out: float32 [768, 768], P('narrow')
- grad_cross_query: float32 [768, 768], P('narrow')
- grad_cross_kv: float32 [768, 1536], P('narrow')
- grad_cross_out: float32 [768, 768], P('narrow')
- grad_mlp_in: float32 [768, 3072], P('narrow')
- grad_mlp_bias_in: float32 [3072], P('narrow')
- grad_mlp_out: float32 [3072, 768], P('narrow')
- grad_mlp_bias_out: float32 [768], P('narrow')
Inputs may be any that keep to these rules, and one draw needn't show every extreme that they name: `image_group`: each image is named by exactly two captions. The captions of one index of wide, an aligned block of 16, name only the 8 images of that index. `caption_len`: in every aligned block of 16 captions one caption has 64 valid tokens and one has 16.
All inputs are finite; a program needn't handle non-finite values.
Results may differ from a plain program's by a relative error of at most 0.033.
Values may be sent and summed in bfloat16 or wider, within the bound.
No kernel may reach another device: no remote copies, remote signals or barrier semaphores. Data moves between devices by JAX's collectives and lax.ppermute only.
A program may use at most 256 MiB of HBM per device.

v0:
```python
import jax
import jax.numpy as jnp
from jax import lax
from jax.sharding import PartitionSpec as P

D = 768
HEADS = 12
HEAD_DIM = 64
SEQ = 64


def joined(value, axis, join):
    pieces = jax.tree.map(lambda part: lax.all_gather(part, axis), value)
    head = jax.tree.map(lambda part: part[0], pieces)
    tail = jax.tree.map(lambda part: part[1:], pieces)
    total, _ = lax.scan(lambda total, section: (join(total, section), None), head, tail)
    return total


def apply_layer_norm(values, gain_row, shift_row):
    center = values - jnp.mean(values, axis=-1, keepdims=True)
    inv_std = lax.rsqrt(jnp.mean(center * center, axis=-1, keepdims=True) + 1e-05)
    normed = center * inv_std
    return (normed * gain_row + shift_row, normed, inv_std)


def layer_norm_backward(grad_norm, normed, inv_std, gain_row):
    scaled = grad_norm * gain_row
    return inv_std * (
        scaled
        - jnp.mean(scaled, axis=-1, keepdims=True)
        - normed * jnp.mean(scaled * normed, axis=-1, keepdims=True)
    )


def mat_mul(left, right):
    return jnp.dot(left, right, preferred_element_type=jnp.float32)


def back_mul(left, right):
    return lax.dot_general(
        left, right, (((1,), (1,)), ((), ())), preferred_element_type=jnp.float32
    )


def outer_mul(left, right):
    return lax.dot_general(
        left, right, (((0,), (0,)), ((), ())), preferred_element_type=jnp.float32
    )


def exact_gelu(values):
    return jax.nn.gelu(values, approximate=False)


def merge_stats(first_part, second_part):
    top_max = jnp.maximum(first_part[0], second_part[0])
    return (
        top_max,
        first_part[1] * jnp.exp(first_part[0] - top_max)
        + second_part[1] * jnp.exp(second_part[0] - top_max),
    )


def masked_probs(queries, keys_low, allowed, score_scale):
    logits = (
        jnp.einsum("cqhd,ckhd->chqk", queries, keys_low, preferred_element_type=jnp.float32)
        * score_scale
    )
    return jax.nn.softmax(jnp.where(allowed, logits, -1e30), axis=-1)


def cross_scores(queries, keys_low, score_scale):
    return (
        jnp.einsum("cqhd,ckhd->chqk", queries, keys_low, preferred_element_type=jnp.float32)
        * score_scale
    )


def local(
    hidden_in,
    image_tokens,
    image_group,
    caption_len,
    norm_gain,
    norm_bias,
    self_qkv,
    self_out,
    cross_query,
    cross_kv,
    cross_out,
    mlp_in,
    mlp_bias_in,
    mlp_out,
    mlp_bias_out,
    out_grad,
):
    tok_rows = hidden_in.shape[0]
    image_count = image_tokens.shape[0]
    image_rows = image_tokens.shape[1]
    narrow_count = lax.axis_size("narrow")
    share_rows = tok_rows // narrow_count
    share_start = lax.axis_index("narrow") * share_rows
    score_scale = HEAD_DIM ** (-0.5)
    layer_norm_gains = norm_gain.astype(jnp.float32)
    layer_norm_shifts = norm_bias.astype(jnp.float32)

    def row_share(values):
        return lax.dynamic_slice_in_dim(values, share_start, share_rows, 0)

    def select_rows(values):
        return row_share(values)

    local_rows = hidden_in.shape[0]
    local_caps = local_rows // SEQ

    def heads_of(values):
        return values.reshape(local_caps, SEQ, HEADS, HEAD_DIM)

    positions = jnp.arange(SEQ)
    allowed = (positions[:, None] >= positions[None, :])[None] & (
        positions[None, None, :] < caption_len[:, None, None]
    )
    allowed = allowed[:, None]
    residual_input = hidden_in.astype(jnp.float32)
    first_normalized_rows, first_centered_scaled, first_inverse_deviation = apply_layer_norm(
        residual_input, layer_norm_gains[0], layer_norm_shifts[0]
    )
    attn_input = first_normalized_rows.astype(jnp.bfloat16)
    qkv_low = (
        mat_mul(attn_input, self_qkv)
        .astype(jnp.bfloat16)
        .reshape(local_caps, SEQ, 3, HEADS, HEAD_DIM)
    )
    self_query = qkv_low[:, :, 0]
    self_keys = qkv_low[:, :, 1]
    self_values = qkv_low[:, :, 2]
    self_probs = masked_probs(self_query, self_keys, allowed, score_scale)
    self_probs_low = self_probs.astype(jnp.bfloat16)
    self_mix = jnp.einsum(
        "chqk,ckhd->cqhd", self_probs_low, self_values, preferred_element_type=jnp.float32
    )
    self_mix_low = self_mix.astype(jnp.bfloat16).reshape(local_rows, D)
    first_residual_stream = residual_input + mat_mul(self_mix_low, self_out)
    second_normalized_rows, second_centered_scaled, second_inverse_deviation = apply_layer_norm(
        first_residual_stream, layer_norm_gains[1], layer_norm_shifts[1]
    )
    cross_input = second_normalized_rows.astype(jnp.bfloat16)
    cross_q_local = heads_of(mat_mul(cross_input, cross_query).astype(jnp.bfloat16))
    image_flat = image_tokens.reshape(image_count * image_rows, D)
    kv_low = (
        mat_mul(image_flat, cross_kv)
        .astype(jnp.bfloat16)
        .reshape(image_count, image_rows, 2, HEADS, HEAD_DIM)
    )
    local_group = image_group - lax.axis_index("wide") * image_count
    image_pick = local_group[:, None] == jnp.arange(image_count)[None, :]
    caption_kv = jnp.einsum(
        "cp,pkshd->ckshd",
        image_pick.astype(jnp.bfloat16),
        kv_low,
        preferred_element_type=jnp.float32,
    ).astype(jnp.bfloat16)
    caption_keys = caption_kv[:, :, 0]
    caption_values = caption_kv[:, :, 1]
    cross_logits = cross_scores(cross_q_local, caption_keys, score_scale)
    local_max = jnp.max(cross_logits, axis=-1)
    local_total = jnp.sum(jnp.exp(cross_logits - local_max[..., None]), axis=-1)
    row_top, row_total = joined((local_max, local_total), "narrow", merge_stats)
    log_total = row_top + jnp.log(row_total)
    cross_probs_low = jnp.exp(cross_logits - log_total[..., None]).astype(jnp.bfloat16)
    numerator = jnp.einsum(
        "chqk,ckhd->cqhd", cross_probs_low, caption_values, preferred_element_type=jnp.float32
    )
    cross_mix = lax.psum(numerator.astype(jnp.bfloat16), "narrow").astype(jnp.float32)
    cross_mix_low = cross_mix.astype(jnp.bfloat16).reshape(local_rows, D)
    second_residual_stream = first_residual_stream + mat_mul(cross_mix_low, cross_out)
    third_normalized_rows, third_centered_scaled, third_inverse_deviation = apply_layer_norm(
        second_residual_stream, layer_norm_gains[2], layer_norm_shifts[2]
    )
    mlp_input = third_normalized_rows.astype(jnp.bfloat16)
    pre_act = mat_mul(mlp_input, mlp_in) + mlp_bias_in.astype(jnp.float32)
    activated, gelu_back = jax.vjp(exact_gelu, pre_act)
    act_low = activated.astype(jnp.bfloat16)
    result = second_residual_stream + (mat_mul(act_low, mlp_out) + mlp_bias_out.astype(jnp.float32))
    upstream_gradient = out_grad.astype(jnp.float32)
    grad_bias_out = jnp.sum(select_rows(upstream_gradient), axis=0)
    grad_w_out = outer_mul(select_rows(act_low), select_rows(out_grad))
    grad_pre_low = gelu_back(back_mul(out_grad, mlp_out))[0].astype(jnp.bfloat16)
    grad_bias_in = jnp.sum(select_rows(grad_pre_low).astype(jnp.float32), axis=0)
    grad_w_in = outer_mul(select_rows(mlp_input), select_rows(grad_pre_low))
    third_norm_gradient = back_mul(grad_pre_low, mlp_in)
    third_norm_gain = jnp.sum(select_rows(third_norm_gradient * third_centered_scaled), axis=0)
    shift_three = jnp.sum(select_rows(third_norm_gradient), axis=0)
    second_residual_gradient = upstream_gradient + layer_norm_backward(
        third_norm_gradient, third_centered_scaled, third_inverse_deviation, layer_norm_gains[2]
    )
    grad_two_low = second_residual_gradient.astype(jnp.bfloat16)
    grad_w_cross_out = outer_mul(select_rows(cross_mix_low), select_rows(grad_two_low))
    grad_cmix_local = heads_of(back_mul(grad_two_low, cross_out).astype(jnp.bfloat16))
    delta_local = jnp.einsum(
        "cqhd,cqhd->chq",
        grad_cmix_local.astype(jnp.float32),
        cross_mix,
        precision=lax.Precision.HIGHEST,
    )
    cross_probs = jnp.exp(
        cross_scores(cross_q_local, caption_keys, score_scale) - log_total[..., None]
    )
    grad_cprobs = jnp.einsum(
        "cqhd,ckhd->chqk", grad_cmix_local, caption_values, preferred_element_type=jnp.float32
    )
    grad_cscore = (cross_probs * (grad_cprobs - delta_local[..., None])).astype(jnp.bfloat16)
    query_part = (
        jnp.einsum("chqk,ckhd->cqhd", grad_cscore, caption_keys, preferred_element_type=jnp.float32)
        * score_scale
    )
    grad_cq_sum = lax.psum(query_part.astype(jnp.bfloat16), "narrow")
    grad_cq_low = grad_cq_sum.reshape(local_rows, D)
    grad_ckeys = (
        jnp.einsum(
            "chqk,cqhd->ckhd", grad_cscore, cross_q_local, preferred_element_type=jnp.float32
        )
        * score_scale
    )
    grad_cvalues = jnp.einsum(
        "chqk,cqhd->ckhd", cross_probs_low, grad_cmix_local, preferred_element_type=jnp.float32
    )
    caption_grads = jnp.stack((grad_ckeys, grad_cvalues), axis=2)
    image_grads = jnp.einsum(
        "cp,ckshd->pkshd",
        image_pick.astype(jnp.float32),
        caption_grads,
        precision=lax.Precision.HIGHEST,
    )
    image_grads_low = image_grads.astype(jnp.bfloat16).reshape(image_count * image_rows, 2 * D)
    grad_w_kv = outer_mul(image_flat, image_grads_low)
    grad_image = back_mul(image_grads_low, cross_kv).reshape(image_count, image_rows, D)
    grad_w_query = outer_mul(select_rows(cross_input), select_rows(grad_cq_low))
    second_norm_gradient = back_mul(grad_cq_low, cross_query)
    second_norm_gain = jnp.sum(select_rows(second_norm_gradient * second_centered_scaled), axis=0)
    shift_two = jnp.sum(select_rows(second_norm_gradient), axis=0)
    first_residual_gradient = second_residual_gradient + layer_norm_backward(
        second_norm_gradient, second_centered_scaled, second_inverse_deviation, layer_norm_gains[1]
    )
    grad_one_low = first_residual_gradient.astype(jnp.bfloat16)
    grad_w_self_out = outer_mul(select_rows(self_mix_low), select_rows(grad_one_low))
    grad_smix = heads_of(back_mul(grad_one_low, self_out).astype(jnp.bfloat16))
    self_probs_again = masked_probs(self_query, self_keys, allowed, score_scale)
    grad_sprobs = jnp.einsum(
        "cqhd,ckhd->chqk", grad_smix, self_values, preferred_element_type=jnp.float32
    )
    self_delta = jnp.einsum(
        "cqhd,cqhd->chq", grad_smix.astype(jnp.float32), self_mix, precision=lax.Precision.HIGHEST
    )
    grad_sscore = (self_probs_again * (grad_sprobs - self_delta[..., None])).astype(jnp.bfloat16)
    self_query_gradient = (
        jnp.einsum("chqk,ckhd->cqhd", grad_sscore, self_keys, preferred_element_type=jnp.float32)
        * score_scale
    )
    self_key_gradient = (
        jnp.einsum("chqk,cqhd->ckhd", grad_sscore, self_query, preferred_element_type=jnp.float32)
        * score_scale
    )
    self_value_gradient = jnp.einsum(
        "chqk,cqhd->ckhd", self_probs_low, grad_smix, preferred_element_type=jnp.float32
    )
    query_key_value_gradient_narrow = jnp.stack(
        (self_query_gradient, self_key_gradient, self_value_gradient), axis=2
    ).astype(jnp.bfloat16)
    query_key_value_gradient_narrow = query_key_value_gradient_narrow.reshape(local_rows, 3 * D)
    grad_w_qkv = outer_mul(select_rows(attn_input), select_rows(query_key_value_gradient_narrow))
    first_norm_gradient = back_mul(query_key_value_gradient_narrow, self_qkv)
    first_norm_gain = jnp.sum(select_rows(first_norm_gradient * first_centered_scaled), axis=0)
    shift_one = jnp.sum(select_rows(first_norm_gradient), axis=0)
    input_gradient = first_residual_gradient + layer_norm_backward(
        first_norm_gradient, first_centered_scaled, first_inverse_deviation, layer_norm_gains[0]
    )
    local_grads = (
        jnp.stack((first_norm_gain, second_norm_gain, third_norm_gain)),
        jnp.stack((shift_one, shift_two, shift_three)),
        grad_w_qkv,
        grad_w_self_out,
        grad_w_query,
        grad_w_kv,
        grad_w_cross_out,
        grad_w_in,
        grad_bias_in,
        grad_w_out,
        grad_bias_out,
    )
    shards = (
        lax.psum_scatter(
            local_grads[0].astype(jnp.bfloat16), "narrow", scatter_dimension=1, tiled=True
        ).astype(jnp.float32),
        lax.psum_scatter(
            local_grads[1].astype(jnp.bfloat16), "narrow", scatter_dimension=1, tiled=True
        ).astype(jnp.float32),
        lax.psum_scatter(
            local_grads[2].astype(jnp.bfloat16), "narrow", scatter_dimension=0, tiled=True
        ).astype(jnp.float32),
        lax.psum_scatter(
            local_grads[3].astype(jnp.bfloat16), "narrow", scatter_dimension=0, tiled=True
        ).astype(jnp.float32),
        lax.psum_scatter(
            local_grads[4].astype(jnp.bfloat16), "narrow", scatter_dimension=0, tiled=True
        ).astype(jnp.float32),
        lax.psum_scatter(
            local_grads[5].astype(jnp.bfloat16), "narrow", scatter_dimension=0, tiled=True
        ).astype(jnp.float32),
        lax.psum_scatter(
            local_grads[6].astype(jnp.bfloat16), "narrow", scatter_dimension=0, tiled=True
        ).astype(jnp.float32),
        lax.psum_scatter(
            local_grads[7].astype(jnp.bfloat16), "narrow", scatter_dimension=0, tiled=True
        ).astype(jnp.float32),
        lax.psum_scatter(
            local_grads[8].astype(jnp.bfloat16), "narrow", scatter_dimension=0, tiled=True
        ).astype(jnp.float32),
        lax.psum_scatter(
            local_grads[9].astype(jnp.bfloat16), "narrow", scatter_dimension=0, tiled=True
        ).astype(jnp.float32),
        lax.psum_scatter(
            local_grads[10].astype(jnp.bfloat16), "narrow", scatter_dimension=0, tiled=True
        ).astype(jnp.float32),
    )
    totals = (
        lax.psum(shards[0].astype(jnp.bfloat16), "wide").astype(jnp.float32),
        lax.psum(shards[1].astype(jnp.bfloat16), "wide").astype(jnp.float32),
        lax.psum(shards[2].astype(jnp.bfloat16), "wide").astype(jnp.float32),
        lax.psum(shards[3].astype(jnp.bfloat16), "wide").astype(jnp.float32),
        lax.psum(shards[4].astype(jnp.bfloat16), "wide").astype(jnp.float32),
        lax.psum(shards[5].astype(jnp.bfloat16), "wide").astype(jnp.float32),
        lax.psum(shards[6].astype(jnp.bfloat16), "wide").astype(jnp.float32),
        lax.psum(shards[7].astype(jnp.bfloat16), "wide").astype(jnp.float32),
        lax.psum(shards[8].astype(jnp.bfloat16), "wide").astype(jnp.float32),
        lax.psum(shards[9].astype(jnp.bfloat16), "wide").astype(jnp.float32),
        lax.psum(shards[10].astype(jnp.bfloat16), "wide").astype(jnp.float32),
    )
    final_out = row_share(result).astype(jnp.bfloat16)
    final_grad = row_share(input_gradient)
    return (
        final_out,
        final_grad,
        grad_image,
        totals[0],
        totals[1],
        totals[2],
        totals[3],
        totals[4],
        totals[5],
        totals[6],
        totals[7],
        totals[8],
        totals[9],
        totals[10],
    )


def solution(mesh):
    in_specs = (
        P("wide", None),
        P("wide", "narrow", None),
        P("wide"),
        P("wide"),
        P(),
        P(),
        P(),
        P(),
        P(),
        P(),
        P(),
        P(),
        P(),
        P(),
        P(),
        P("wide", None),
    )
    out_specs = (
        P(("wide", "narrow"), None),
        P(("wide", "narrow"), None),
        P("wide", "narrow", None),
        P(None, "narrow"),
        P(None, "narrow"),
        P("narrow", None),
        P("narrow", None),
        P("narrow", None),
        P("narrow", None),
        P("narrow", None),
        P("narrow", None),
        P("narrow"),
        P("narrow", None),
        P("narrow"),
    )
    return jax.shard_map(local, mesh=mesh, in_specs=in_specs, out_specs=out_specs, check_vma=False)
```

profile of v0, /device:TPU:0, one launch (start us, length us, event | category | flops | bytes accessed | tf_op | source)
XLA Modules:
  0.0 967.1 jit_solution(15664913174151155731)
XLA Ops:
  17.8 5.5 convolution_convert_fusion
  23.3 6.6 copy.169
  29.9 13.2 %reshape.198 = bf16[16,64,3,12,64]{1,0,4,3,2:T(8,128)(2,1)} reshape(bf16[1024,2304]{0,1:T(8,128)(2,1)} %copy.169) | data formatting | bytes 9437184 | tf_op jit(solution)/shard_map/reshape | solution.py:133
  43.1 6.5 fusion.120
  49.6 5.1 copy.252
  54.6 5.0 copy.253
  60.4 4.6 fusion.22
  68.2 4.7 bitcast_convert_fusion
  72.8 4.2 copy.174
  77.0 5.4 reshape.199
  82.4 3.7 fusion.122
  92.8 5.9 reshape.240
  98.6 6.5 copy.209
  105.2 6.4 convolution_convert_fusion.4
  111.6 4.8 copy.175
  116.4 4.4 copy.256
  126.7 3.6 multiply_reduce_fusion.1
  130.4 3.6 exponential_reduce_fusion
  134.1 6.4 all-gather.1
  140.4 5.3 all-gather
  146.5 3.9 convert_bitcast_fusion.1
  153.9 84.0 %all-reduce.9.cloned.1.call-done = bf16[16,64,12,64]{1,3,2,0:T(8,128)(2,1)} async-done(((bf16[16,64,12,64]{1,3,2,0:T(8,128)(2,1)}), bf16[16,64,12,64]{1,3,2,0:T(8,128)(2,1)}) %all-reduce.9.cloned.1.call-update) | async-done | bytes 1572880 | tf_op jit(solution)/shard_map/psum | solution.py:175
  237.9 6.0 copy.183
  243.9 5.4 reshape.203
  249.3 4.2 fusion.123
  256.4 36.9 %multiply_convert_fusion = (bf16[1024,3072]{1,0:T(8,128)(2,1)}, f32[1024,3072]{1,0:T(8,128)}, f32[1024,3072]{1,0:T(8,128)}) fusion(f32[3072]{0:T(1024)S(1)} %convert_element_type.202, bf16[1024,768]{0,1:T(8,128)(2,1)S(1)} %get-tuple-element.115, bf16[768,3072]{1,0:T(8,128)(2,1)} %param.27), kind=kOutput, calls=%fused_computation.7 | convolution fusion | flops 5039456256 | bytes 37761024 | tf_op jit(solution)/shard_map/dot_general | solution.py:37
  293.3 16.7 %add_convert_fusion = bf16[1024,3072]{1,0:T(8,128)(2,1)} fusion(f32[1024,3072]{1,0:T(8,128)} %get-tuple-element.114, f32[1024,3072]{1,0:T(8,128)} %get-tuple-element.138, f32[3072]{0:T(1024)S(1)} %convert_element_type.202, bf16[1024,768]{1,0:T(8,128)(2,1)S(1)} %copy-done.33, bf16[3072,768]{1,0:T(8,128)(2,1)} %param.29), kind=kOutput, calls=%fused_computation.6 | convolution fusion | flops 4879024128 | bytes 37761024 | tf_op jit(solution)/shard_map/dot_general | solution.py:41
  310.0 9.7 %fusion.125 = f32[1024,768]{1,0:T(8,128)} fusion(bf16[1024,3072]{1,0:T(8,128)(2,1)} %add_convert_fusion, bf16[768,3072]{1,0:T(8,128)(2,1)} %param.27), kind=kOutput, calls=%fused_computation.203 | convolution fusion | flops 4831838208 | bytes 14155776 | tf_op jit(solution)/shard_map/dot_general | solution.py:41
  319.7 3.6 copy.186
  336.9 5.2 reshape.204
  344.9 6.6 fusion.53
  354.9 7.1 multiply_convert_fusion.5
  369.2 5.2 copy.192
  374.5 5.4 reshape.205
  379.9 11.9 %pad_maximum_fusion = f32[16,128,2,12,64]{1,4,3,0,2:T(8,128)} fusion(f32[16,128,1,12,64]{1,4,3,0,2:T(8,128)} %fusion.53, f32[16,128,1,12,64]{1,4,3,0,2:T(8,128)} %multiply_bitcast_fusion), kind=kLoop, calls=%fused_computation.3 | loop fusion | flops 3145728 | bytes 25165824 | tf_op jit(solution)/shard_map/stack | solution.py:229
  391.9 16.2 %fusion.71 = bf16[8,128,2,12,64]{1,0,4,3,2:T(8,128)(2,1)S(1)} fusion(f32[16,128,2,12,64]{1,4,3,0,2:T(8,128)} %pad_maximum_fusion, s32[16]{0:T(128)S(1)} %copy-done.64), kind=kOutput, calls=%fused_computation.115 | convolution fusion | flops 303562880 | bytes 15728704 | tf_op jit(solution)/shard_map/cp,ckshd->pkshd/dot_general | solution.py:230
  409.8 3.8 fusion.33
  413.6 4.3 copy.249
  421.3 10.2 %all-reduce.11.cloned.1.call-done = bf16[1024,768]{0,1:T(8,128)(2,1)} async-done(((bf16[1024,768]{0,1:T(8,128)(2,1)}), bf16[1024,768]{0,1:T(8,128)(2,1)}) %all-reduce.11.cloned.1.call-update) | async-done | bytes 1572880 | tf_op jit(solution)/shard_map/psum | solution.py:218
  431.5 4.8 fusion.126
  436.4 4.1 copy.193
  445.2 5.4 fusion.118
  457.0 5.2 reshape.206
  465.4 5.2 bitcast_convert_fusion.1
  473.9 8.1 fusion.9
  482.1 6.8 multiply_convert_fusion.3
  493.3 5.8 fusion.16
  499.2 6.9 convert_bitcast_fusion
  506.1 9.7 %pad_maximum_fusion.1 = bf16[16,64,3,12,64]{4,1,3,0,2:T(8,128)(2,1)} fusion(bf16[16,64,1,12,64]{4,1,3,0,2:T(8,128)(2,1)} %convert_bitcast_fusion, bf16[16,64,1,12,64]{4,1,3,0,2:T(8,128)(2,1)} %fusion.17, bf16[16,64,1,12,64]{4,1,3,0,2:T(8,128)(2,1)} %fusion.16), kind=kLoop, calls=%fused_computation.21 | loop fusion | flops 4718592 | bytes 9437184 | tf_op jit(solution)/shard_map/stack | solution.py:268
  515.8 13.5 %copy.207 = bf16[16,64,3,12,64]{1,0,4,3,2:T(8,128)(2,1)} copy(bf16[16,64,3,12,64]{4,1,3,0,2:T(8,128)(2,1)} %pad_maximum_fusion.1) | data formatting | bytes 9437184 | tf_op jit(solution)/shard_map/stack | solution.py:268
  529.2 13.3 %convert_element_type.216 = bf16[1024,2304]{0,1:T(8,128)(2,1)} reshape(bf16[16,64,3,12,64]{1,0,4,3,2:T(8,128)(2,1)} %copy.207) | data formatting | bytes 9437184 | tf_op jit(solution)/shard_map/convert_element_type | solution.py:270
  542.6 5.7 convolution_convert_fusion.3
  548.6 7.5 convolution_convert_fusion.2
  556.1 6.9 convolution_convert_fusion.1
  568.7 7.8 fusion.127
  576.5 3.6 copy.208
  598.8 60.6 %reduce-scatter.24.cloned.1.call-done = bf16[384,3072]{1,0:T(8,128)(2,1)} async-done(((bf16[768,3072]{1,0:T(8,128)(2,1)}), bf16[384,3072]{1,0:T(8,128)(2,1)}) %reduce-scatter.24.cloned.1.call-update) | async-done | bytes 2359312 | tf_op jit(solution)/shard_map/reduce_scatter | solution.py:314
  659.4 62.3 %reduce-scatter.26.cloned.1.call-done = bf16[1536,768]{1,0:T(8,128)(2,1)} async-done(((bf16[3072,768]{1,0:T(8,128)(2,1)}), bf16[1536,768]{1,0:T(8,128)(2,1)}) %reduce-scatter.26.cloned.1.call-update) | async-done | bytes 2359312 | tf_op jit(solution)/shard_map/reduce_scatter | solution.py:320
  728.7 8.8 fusion.124
  743.5 5.6 all-reduce.4
  750.5 7.0 fusion.27
  762.5 63.8 %all-reduce.2 = (bf16[3,384]{1,0:T(4,128)(2,1)}, bf16[3,384]{1,0:T(4,128)(2,1)}, bf16[1536]{0:T(1024)(128)(2,1)S(1)}, bf16[384]{0:T(512)(128)(2,1)}) all-reduce(bf16[3,384]{1,0:T(4,128)(2,1)S(1)} %copy.246, bf16[3,384]{1,0:T(4,128)(2,1)S(1)} %copy.248, ...), channel_id=1, replica_groups=mesh['wide'=16,'narrow'=2] {'wide'}, use_global_device_ids=true, to_apply=%region_22.23 | all-reduce | flops 4224 | bytes 16896 | tf_op jit(solution)/shard_map/psum | solution.py:328
  830.8 111.7 %all-reduce.13.cloned.1.call-done = (bf16[384,1536]{0,1:T(8,128)(2,1)}, bf16[384,2304]{1,0:T(8,128)(2,1)}, bf16[384,768]{1,0:T(8,128)(2,1)}, bf16[384,768]{1,0:T...) async-done(((bf16[384,1536]{0,1:T(8,128)(2,1)}, bf16[384,2304]{1,0:T(8,128)(2,1)}, bf16[384,768]{1,0:T(8,128)(2,1)}, ...) | async-done | bytes 9437200 | tf_op jit(solution)/shard_map/psum | solution.py:333
  942.5 4.6 convert_element_type.232
  (283 shorter events, 147.6 us)
Async XLA Ops:
  7.2 10.6 %copy-start = (bf16[768,2304]{1,0:T(8,128)(2,1)S(1)}, bf16[768,2304]{1,0:T(8,128)(2,1)}, u32[]{:S(2)}) copy-start(bf16[768,2304]{1,0:T(8,128)(2,1)} %param.22) | copy-start | bytes 10616836
  7.2 230.7 %all-reduce.9.cloned.1.call-start = ((), (), s32[]{:S(2)}) async-start(), calls=%async_computation.9 | async-start | bytes 6291456 | tf_op jit(solution)/shard_map/psum | solution.py:175
  7.3 6.4 copy-start.61
  10.0 3.7 copy-start.62
  10.0 4.4 copy-start.6
  11.8 4.8 copy-start.42
  14.4 72.2 %copy-start.46 = (f32[768]{0:T(1024)}, f32[768]{0:T(1024)S(1)}, u32[]{:S(2)}) copy-start(f32[768]{0:T(1024)S(1)} %get-tuple-element.140) | copy-start | bytes 9220
  14.4 239.6 %copy-start.40 = (f32[768]{0:T(1024)}, f32[768]{0:T(1024)S(1)}, u32[]{:S(2)}) copy-start(f32[768]{0:T(1024)S(1)} %get-tuple-element.141) | copy-start | bytes 9220
  68.1 4.7 copy-start.72
  68.1 4.7 copy-start.73
  86.9 3.3 copy-start.68
  116.4 4.4 copy-start.70
  126.5 3.8 copy-start.11
  126.5 19.4 %copy-start.21 = (bf16[16,128,12,64]{1,0,3,2:T(8,128)(2,1)}, bf16[16,128,12,64]{1,0,3,2:T(8,128)(2,1)S(1)}, u32[]{:S(2)}) copy-start(bf16[16,128,12,64]{1,0,3,2:T(8,128)(2,1)S(1)} %get-tuple-element.123) | copy-start | bytes 9437188
  130.3 15.5 %copy-start.1 = (f32[16,12,64,128]{3,2,1,0:T(8,128)}, f32[16,12,64,128]{3,2,1,0:T(8,128)S(1)}, u32[]{:S(2)}) copy-start(f32[16,12,64,128]{3,2,1,0:T(8,128)S(1)} %get-tuple-element.135) | copy-start | bytes 18874372
  150.4 281.1 %all-reduce.11.cloned.1.call-start = ((), (), s32[]{:S(2)}) async-start(), calls=%async_computation.10 | async-start | bytes 3145728 | tf_op jit(solution)/shard_map/psum | solution.py:218
  256.4 36.9 %copy-start.36 = (bf16[1024,768]{0,1:T(8,128)(2,1)}, bf16[1024,768]{0,1:T(8,128)(2,1)S(1)}, u32[]{:S(2)}) copy-start(bf16[1024,768]{0,1:T(8,128)(2,1)S(1)} %get-tuple-element.115) | copy-start | bytes 4718596
  256.4 36.9 %copy-start.33 = (bf16[1024,768]{1,0:T(8,128)(2,1)S(1)}, bf16[1024,768]{1,0:T(8,128)(2,1)}, u32[]{:S(2)}) copy-start(bf16[1024,768]{1,0:T(8,128)(2,1)} %param.31) | copy-start | bytes 4718596
  319.7 3.6 copy-start.41
  323.3 3.7 copy-start.2
  323.3 4.7 copy-start.4
  323.3 4.7 copy-start.45
  328.0 3.6 copy-start.67
  342.1 12.8 %slice-start = ((s8[6291456]{0:T(1024)(128)(4,1)}), s8[4194304]{0:T(1024)(128)(4,1)S(1)}, s32[]{:S(2)}) async-start(s8[6291456]{0:T(1024)(128)(4,1)} %bitcast.152), calls=%async_computation.21 | async-start | bytes 8388608
  344.9 6.6 copy-start.18
  344.9 9.9 %slice-start.1 = ((s8[6291456]{0:T(1024)(128)(4,1)}), s8[2097152]{0:T(1024)(128)(4,1)S(1)}, s32[]{:S(2)}) async-start(s8[6291456]{0:T(1024)(128)(4,1)} %bitcast.152), calls=%async_computation.22 | async-start | bytes 4194304
  351.6 3.3 copy-start.22
  354.9 7.2 copy-start.9
  362.1 3.6 copy-start.12
  379.9 12.0 %copy-start.64 = (s32[16]{0:T(128)S(1)}, s32[16]{0:T(128)}, u32[]{:S(2)}) copy-start(s32[16]{0:T(128)} %copy-done.63) | copy-start | bytes 196
  379.9 216.5 %reduce-scatter.32.cloned.1.call-start = ((), (), s32[]{:S(2)}) async-start(), calls=%async_computation.19 | async-start | bytes 3538944
  391.9 17.9 %copy-start.66 = (bf16[8,128,768]{2,1,0:T(8,128)(2,1)S(1)}, bf16[8,128,768]{2,1,0:T(8,128)(2,1)}, u32[]{:S(2)}) copy-start(bf16[8,128,768]{2,1,0:T(8,128)(2,1)} %param.17) | copy-start | bytes 4718596
  418.0 180.8 %reduce-scatter.22.cloned.1.call-start = ((), (), s32[]{:S(2)}) async-start(), calls=%async_computation.14 | async-start | bytes 1769472 | tf_op jit(solution)/shard_map/reduce_scatter | solution.py:311
  421.2 177.5 %reduce-scatter.20.cloned.1.call-start = ((), (), s32[]{:S(2)}) async-start(), calls=%async_computation.13 | async-start | bytes 1769472 | tf_op jit(solution)/shard_map/reduce_scatter | solution.py:305
  436.4 4.1 copy-start.47
  440.4 3.8 copy-start.3
  440.4 4.7 copy-start.5
  440.4 4.7 copy-start.53
  440.5 4.7 copy-start.55
  445.2 6.7 copy-start.69
  470.6 128.1 %reduce-scatter.18.cloned.1.call-start = ((), (), s32[]{:S(2)}) async-start(), calls=%async_computation.12 | async-start | bytes 1769472 | tf_op jit(solution)/shard_map/reduce_scatter | solution.py:302
  473.9 8.1 copy-start.19
  473.9 8.2 copy-start.27
  473.9 8.2 copy-start.74
  482.0 8.6 copy-start.10
  493.3 105.5 %reduce-scatter.16.cloned.1.call-start = ((), (), s32[]{:S(2)}) async-start(), calls=%async_computation.11 | async-start | bytes 5308416 | tf_op jit(solution)/shard_map/reduce_scatter | solution.py:299
  493.3 5.9 copy-start.20
  493.3 5.9 copy-start.75
  548.3 111.0 %reduce-scatter.24.cloned.1.call-start = ((), (), s32[]{:S(2)}) async-start(), calls=%async_computation.15 | async-start | bytes 7077888 | tf_op jit(solution)/shard_map/reduce_scatter | solution.py:314
  556.1 165.6 %reduce-scatter.26.cloned.1.call-start = ((), (), s32[]{:S(2)}) async-start(), calls=%async_computation.16 | async-start | bytes 7077888 | tf_op jit(solution)/shard_map/reduce_scatter | solution.py:320
  563.0 197.5 %reduce-scatter.30.cloned.1.call-start = ((), (), s32[]{:S(2)}) async-start(), calls=%async_computation.18 | async-start | bytes 294912
  580.2 3.1 copy-start.59
  580.2 8.3 copy-start.43
  580.2 8.3 copy-start.51
  585.4 6.0 copy-start.25
  588.4 3.9 copy-start.24
  588.4 3.9 copy-start.60
  594.4 167.1 %reduce-scatter.28.cloned.1.call-start = ((), (), s32[]{:S(2)}) async-start(), calls=%async_computation.17 | async-start | bytes 294912
  596.1 346.4 %all-reduce.13.cloned.1.call-start = ((), (), s32[]{:S(2)}) async-start(), calls=%async_computation.20 | async-start | bytes 18874368 | tf_op jit(solution)/shard_map/psum | solution.py:333
  721.7 3.5 copy-start.71
  721.8 5.4 copy-start.65
  728.7 8.8 copy-start.16
  942.5 4.6 copy-start.29
  954.3 4.4 copy-start.39
  (26 other events, 51.1 us)
Sparse Core Ops, SparseCore 0:
  150.5 87.3 all-reduce.8
  380.0 51.4 all-reduce.10
  433.8 34.7 reduce-scatter.31
  470.7 21.7 reduce-scatter.21
  495.2 21.7 reduce-scatter.19
  519.7 21.7 reduce-scatter.17
  548.4 47.8 reduce-scatter.15
  599.3 59.9 reduce-scatter.23
  661.7 59.9 reduce-scatter.25
  723.9 10.9 reduce-scatter.29
  737.7 11.0 reduce-scatter.27
  754.5 187.8 all-reduce.12
where the time goes:
time: 976 us; the launch traced here: 967 us
  waiting for transfers between devices  329 us (34%)
  matrix products  232 us (24%)
  local copies, waits for them, and re-layouts  189 us (19%)
  other arithmetic  118 us (12%)
  blocking collectives  81.1 us (8%)
  between operations  16.8 us (2%)
    psum x1, waiting for transfers between devices, local(): lax.psum(shards[5].astype(jnp.bfloat16), 'wide').astype(jnp.float32)  112 us
    psum x1, waiting for transfers between devices, local(): lax.psum(numerator.astype(jnp.bfloat16), 'narrow').astype(jnp.float32)  84 us
    dot_general x7, matrix products, mat_mul(): return jnp.dot(left, right, preferred_element_type=jnp.float32)  68.1 us
    psum x1, blocking collectives, local(): lax.psum(shards[0].astype(jnp.bfloat16), 'wide').astype(jnp.float32)  63.8 us
    reduce_scatter x1, waiting for transfers between devices, local(): lax.psum_scatter(local_grads[9].astype(jnp.bfloat16), 'narrow', scatter_d...  62.3 us
    reduce_scatter x1, waiting for transfers between devices, local(): lax.psum_scatter(local_grads[7].astype(jnp.bfloat16), 'narrow', scatter_d...  60.6 us
    unnamed x173, local copies, waits for them, and re-layouts  55.3 us
    dot_general x7, matrix products, back_mul(): lax.dot_general(left, right, (((1,), (1,)), ((), ())), preferred_element_...  51.2 us
  transfers between devices with their start and end apart: 12, of which 5 were waited for; matrix products, arithmetic and copies ran while one was open for 25% of the time, Pallas kernels for 0%

commit v1 on v0

v1 whole, which is shorter than its diff:
```python
import functools

import jax
import jax.numpy as jnp
from jax import lax
from jax.experimental import pallas as pl
from jax.experimental.pallas import tpu as pltpu
from jax.sharding import PartitionSpec as P

D = 768
HEADS = 12
HEAD_DIM = 64
FF = 3072
SEQ = 64
IMG_TOK = 256
PAIRS = HEADS // 2
SCALE = HEAD_DIM**-0.5
BLOCK = 48
BLOCKS = D // BLOCK
WIDE_COLS = 2 * D
TILE = 256
f32 = jnp.float32
bf16 = jnp.bfloat16
VM = pl.BlockSpec(memory_space=pltpu.VMEM)
SM = pl.BlockSpec(memory_space=pltpu.SMEM)
CAPS, LENS, MINE, PEER, IMG_SRC, OUT_SRC, FLIP, CORE, PLAN = 0, 8, 16, 20, 24, 32, 40, 41, 48


def mm(left, right):
    return lax.dot_general(left, right, (((1,), (0,)), ((), ())), preferred_element_type=f32)


def mm_nt(left, right):
    return lax.dot_general(left, right, (((1,), (1,)), ((), ())), preferred_element_type=f32)


def mm_tn(left, right):
    return lax.dot_general(left, right, (((0,), (0,)), ((), ())), preferred_element_type=f32)


def params(vmem=56, grid=None):
    return pltpu.CompilerParams(
        vmem_limit_bytes=vmem * 1024 * 1024,
        dimension_semantics=None if grid is None else ("arbitrary",) * grid,
    )


def cost(flops, nbytes, trans=0):
    return pl.CostEstimate(flops=int(flops), bytes_accessed=int(nbytes), transcendentals=int(trans))


def sds(shape, dtype):
    return jax.ShapeDtypeStruct(shape, dtype)


def normed(x):
    center = x - jnp.mean(x, axis=-1, keepdims=True)
    inv = lax.rsqrt(jnp.mean(center * center, axis=-1, keepdims=True) + 1e-05)
    return center * inv, inv


def norm_back(grad, xhat, inv, gain):
    u = grad * gain
    return inv * (
        u - jnp.mean(u, axis=-1, keepdims=True) - xhat * jnp.mean(u * xhat, axis=-1, keepdims=True)
    )


def lane_masks(scale):
    lane = lax.broadcasted_iota(jnp.int32, (1, 2 * HEAD_DIM), 1)
    low = jnp.where(lane < HEAD_DIM, scale, 0.0).astype(bf16)
    high = jnp.where(lane < HEAD_DIM, 0.0, scale).astype(bf16)
    return low, high


def two_heads(x, masks):
    return jnp.concatenate([x * masks[0], x * masks[1]], axis=0)


def join_heads(x, rows):
    lane = lax.broadcasted_iota(jnp.int32, (rows, 2 * HEAD_DIM), 1)
    return jnp.where(lane < HEAD_DIM, x[:rows], x[rows:])


def plan_kernel(narrow, images, group, lens, pos, out, place, count):
    me = pos[0]
    base = pos[1]
    half = images // narrow
    caps = 2 * images
    for p in range(images):
        count[p] = 0
    for c in range(caps):
        g = group[c] - base
        n = count[g]
        place[2 * g + n] = c
        count[g] = n + 1
    for i in range(PLAN):
        out[i] = 0
    out[FLIP] = pos[2]
    out[CORE] = pos[3]
    slots = [jnp.int32(0) for _ in range(2)]
    turn = jnp.int32(0)
    for p in range(images):
        a = place[2 * p]
        b = place[2 * p + 1]
        if narrow == 2:
            both_low = b < images
            both_high = a >= images
            mixed = jnp.logical_not(jnp.logical_or(both_low, both_high))
            owner = jnp.where(both_low, 0, jnp.where(both_high, 1, turn))
            turn = jnp.where(mixed, 1 - turn, turn)
            slot = jnp.where(owner == 0, slots[0], slots[1])
            slots[0] = jnp.where(owner == 0, slots[0] + 1, slots[0])
            slots[1] = jnp.where(owner == 1, slots[1] + 1, slots[1])
            swap = jnp.logical_and(mixed, owner == 1)
            first = jnp.where(swap, b, a)
            second = jnp.where(swap, a, b)
            mine = owner == me

            @pl.when(mine)
            def _():
                out[MINE + slot] = p
                out[CAPS + 2 * slot] = first
                out[CAPS + 2 * slot + 1] = second
                out[LENS + 2 * slot] = lens[first]
                out[LENS + 2 * slot + 1] = lens[second]

            @pl.when(jnp.logical_not(mine))
            def _():
                out[PEER + slot] = p

            out[IMG_SRC + p] = jnp.where(mine, slot, half + slot)
            for k, c in ((0, first), (1, second)):

                @pl.when(c // images == me)
                def _():
                    out[OUT_SRC + c - me * images] = jnp.where(mine, 2 * slot + k, caps // 2 + slot)

        else:
            owner = p // half
            slot = p % half
            mine = owner == me
            per = caps // narrow

            @pl.when(mine)
            def _():
                out[MINE + slot] = p
                for k, c in ((0, a), (1, b)):
                    out[CAPS + 2 * slot + k] = c
                    out[LENS + 2 * slot + k] = lens[c]

            for k, c in ((0, a), (1, b)):

                @pl.when(c // per == me)
                def _():
                    out[OUT_SRC + c - me * per] = 2 * p + k


def make_plan(narrow, images, group, lens, pos):
    return pl.pallas_call(
        functools.partial(plan_kernel, narrow, images),
        out_shape=sds((PLAN,), jnp.int32),
        in_specs=[SM, SM, SM],
        out_specs=SM,
        scratch_shapes=[
            pltpu.SMEM((2 * images,), jnp.int32),
            pltpu.SMEM((images,), jnp.int32),
        ],
        compiler_params=params(4),
        name="plan",
    )(group, lens, pos)


def pick_kernel(plan, tokens_a, tokens_b, mine, peer):
    mine[...] = tokens_a[...]
    peer[...] = tokens_b[...]


def pick_tokens(plan, tokens, count):
    block = (1,) + tokens.shape[1:]
    return pl.pallas_call(
        pick_kernel,
        grid_spec=pltpu.PrefetchScalarGridSpec(
            num_scalar_prefetch=1,
            grid=(count,),
            in_specs=[
                pl.BlockSpec(block, lambda i, plan: (plan[MINE + i], 0, 0)),
                pl.BlockSpec(block, lambda i, plan: (plan[PEER + i], 0, 0)),
            ],
            out_specs=[pl.BlockSpec(block, lambda i, plan: (i, 0, 0))] * 2,
        ),
        out_shape=[sds((count,) + tokens.shape[1:], bf16)] * 2,
        compiler_params=params(8),
        name="pick",
    )(plan, tokens, tokens)


def place_kernel(offset, count, plan, own, got, out):
    have = own.shape[0]
    for i in range(count):
        src = plan[offset + i]

        @pl.when(src < have)
        def _():
            out[i] = own[jnp.minimum(src, have - 1)].astype(out.dtype)

        @pl.when(src >= have)
        def _():
            out[i] = got[jnp.maximum(src - have, 0)].astype(out.dtype)


def place(offset, count, plan, own, got, dtype, name):
    return pl.pallas_call(
        functools.partial(place_kernel, offset, count),
        out_shape=sds((count,) + own.shape[1:], dtype),
        in_specs=[SM, VM, VM],
        out_specs=VM,
        compiler_params=params(24),
        cost_estimate=cost(0, 4 * count * own.shape[1] * own.shape[2] * 2),
        name=name,
    )(plan, own, got)


def front_kernel(
    plan, hidden, out_grad, gain, bias, w_qkv, w_self, w_query,
    x_out, g_out, attn_out, qkv_out, probs_out, mix_out, one_out, cin_out, cq_out,
):
    rows = x_out.shape[0]
    gain0, bias0 = gain[0:1, :].astype(f32), bias[0:1, :].astype(f32)
    gain1, bias1 = gain[1:2, :].astype(f32), bias[1:2, :].astype(f32)

    def gather(i, _):
        src = pl.ds(pl.multiple_of(plan[CAPS + i] * SEQ, SEQ), SEQ)
        dst = pl.ds(pl.multiple_of(i * SEQ, SEQ), SEQ)
        x = hidden[src, :]
        x_out[dst, :] = x
        g_out[dst, :] = out_grad[src, :]
        attn_out[dst, :] = (normed(x.astype(f32))[0] * gain0 + bias0).astype(bf16)
        return 0

    lax.fori_loop(0, rows // SEQ, gather, 0)
    for j in range(3):
        cols = slice(j * D, (j + 1) * D)
        qkv_out[:, cols] = mm(attn_out[...], w_qkv[:, cols]).astype(bf16)
    masks = lane_masks(SCALE)
    row = lax.broadcasted_iota(jnp.int32, (2 * SEQ, 2 * SEQ), 0)
    col = lax.broadcasted_iota(jnp.int32, (2 * SEQ, 2 * SEQ), 1)
    causal = jnp.logical_and(col <= row, (col // SEQ) == (row // SEQ))

    def attend(p, _):
        span = pl.ds(pl.multiple_of(p * 2 * SEQ, 2 * SEQ), 2 * SEQ)
        length = jnp.where(col < SEQ, plan[LENS + 2 * p], plan[LENS + 2 * p + 1])
        allowed = jnp.logical_and(causal, (col % SEQ) < length)
        fill = jnp.where(allowed, 0.0, -1e30)
        fill = jnp.concatenate([fill, fill], axis=0)
        for h in range(PAIRS):
            at = 2 * HEAD_DIM * h
            q = two_heads(qkv_out[span, at : at + 128], masks)
            k = qkv_out[span, D + at : D + at + 128]
            v = qkv_out[span, 2 * D + at : 2 * D + at + 128]
            logits = jnp.where(fill < 0.0, fill, mm_nt(q, k))
            e = jnp.exp(logits - jnp.max(logits, axis=-1, keepdims=True))
            low = (e * (1.0 / jnp.sum(e, axis=-1, keepdims=True))).astype(bf16)
            probs_out[p, h] = low
            mix_out[span, at : at + 128] = join_heads(mm(low, v), 2 * SEQ).astype(bf16)
        return 0

    lax.fori_loop(0, rows // (2 * SEQ), attend, 0)
    one_out[...] = mm(mix_out[...], w_self[...])

    def second(i, _):
        span = pl.ds(pl.multiple_of(i * SEQ, SEQ), SEQ)
        one = one_out[span, :] + x_out[span, :].astype(f32)
        one_out[span, :] = one
        cin_out[span, :] = (normed(one)[0] * gain1 + bias1).astype(bf16)
        return 0

    lax.fori_loop(0, rows // SEQ, second, 0)
    cq_out[...] = mm(cin_out[...], w_query[...]).astype(bf16)


def front(rows, plan, hidden, out_grad, gain, bias, w_qkv, w_self, w_query):
    pairs = rows // (2 * SEQ)
    return pl.pallas_call(
        front_kernel,
        out_shape=[
            sds((rows, D), bf16),
            sds((rows, D), bf16),
            sds((rows, D), bf16),
            sds((rows, 3 * D), bf16),
            sds((pairs, PAIRS, 4 * SEQ, 2 * SEQ), bf16),
            sds((rows, D), bf16),
            sds((rows, D), f32),
            sds((rows, D), bf16),
            sds((rows, D), bf16),
        ],
        in_specs=[SM] + [VM] * 7,
        out_specs=[VM] * 9,
        compiler_params=params(),
        cost_estimate=cost(rows * D * D * 10 * 2, 24e6, rows * 2 * D),
        name="front",
    )(plan, hidden, out_grad, gain, bias, w_qkv, w_self, w_query)


def cross_kernel(tokens, cq, one, gain, bias, w_kv, w_cross, kv_out, probs_out, mix_out, two_out, min_out):
    rows = cq.shape[0]
    images = rows // (2 * SEQ)
    gain2, bias2 = gain[2:3, :].astype(f32), bias[2:3, :].astype(f32)
    for j in range(2):
        cols = slice(j * D, (j + 1) * D)
        kv_out[:, cols] = mm(tokens[...], w_kv[:, cols]).astype(bf16)
    masks = lane_masks(SCALE)

    def attend(p, _):
        span = pl.ds(pl.multiple_of(p * 2 * SEQ, 2 * SEQ), 2 * SEQ)
        toks = pl.ds(pl.multiple_of(p * IMG_TOK, IMG_TOK), IMG_TOK)
        for h in range(PAIRS):
            at = 2 * HEAD_DIM * h
            q = two_heads(cq[span, at : at + 128], masks)
            logits = mm_nt(q, kv_out[toks, at : at + 128])
            e = jnp.exp(logits - jnp.max(logits, axis=-1, keepdims=True))
            low = (e * (1.0 / jnp.sum(e, axis=-1, keepdims=True))).astype(bf16)
            probs_out[p, h] = low
            mix = mm(low, kv_out[toks, D + at : D + at + 128])
            mix_out[span, at : at + 128] = join_heads(mix, 2 * SEQ).astype(bf16)
        return 0

    lax.fori_loop(0, images, attend, 0)
    two_out[...] = mm(mix_out[...], w_cross[...])

    def second(i, _):
        span = pl.ds(pl.multiple_of(i * SEQ, SEQ), SEQ)
        two = two_out[span, :] + one[span, :]
        two_out[span, :] = two
        min_out[span, :] = (normed(two)[0] * gain2 + bias2).astype(bf16)
        return 0

    lax.fori_loop(0, rows // SEQ, second, 0)


def cross(tokens, cq, one, gain, bias, w_kv, w_cross):
    rows = cq.shape[0]
    images = rows // (2 * SEQ)
    return pl.pallas_call(
        cross_kernel,
        out_shape=[
            sds((tokens.shape[0], 2 * D), bf16),
            sds((images, PAIRS, 4 * SEQ, IMG_TOK), bf16),
            sds((rows, D), bf16),
            sds((rows, D), f32),
            sds((rows, D), bf16),
        ],
        in_specs=[VM] * 7,
        out_specs=[VM] * 5,
        compiler_params=params(),
        cost_estimate=cost(rows * D * D * 8 * 2, 20e6, rows * 4 * D),
        name="cross",
    )(tokens, cq, one, gain, bias, w_kv, w_cross)


def store_split(core, keep, send, first, second):
    @pl.when(core == 0)
    def _():
        first(keep)
        second(send)

    @pl.when(core == 1)
    def _():
        first(send)
        second(keep)


def mlp_kernel(
    plan, min_ref, g_ref, acc_in, gn_in, w_in, b_in, w_out,
    acc, gn, keep, send, gbias, min_t,
):
    step = pl.program_id(0)
    flip = plan[FLIP]

    @pl.when(step == 0)
    def _():
        acc[...] = acc_in[...]
        gn[...] = gn_in[...]
        min_t[...] = min_ref[...].T

    pre = mm(min_ref[...], w_in[...]) + b_in[...].astype(f32)
    phi = 0.5 + 0.5 * lax.erf(pre * (2.0**-0.5))
    act = (pre * phi).astype(bf16)
    slope = phi + pre * jnp.exp(-0.5 * pre * pre) * 0.3989422804014327
    acc[...] += mm(act, w_out[...])
    grad_pre = slope * mm_nt(g_ref[...], w_out[...])
    gbias[...] = jnp.sum(grad_pre, axis=0, keepdims=True)
    low = grad_pre.astype(bf16)
    gn[...] += mm_nt(low, w_in[...])
    grad_in = mm(min_t[...], low).astype(bf16)
    grad_out = mm_tn(act, g_ref[...]).astype(bf16)
    cols = pl.ds(pl.multiple_of(step * TILE, TILE), TILE)
    half = step // 3
    spot = pl.ds(pl.multiple_of((step % 3) * 16, 16), 16)

    def first(ref):
        for b in range(BLOCKS):
            ref[b ^ flip, :, cols] = grad_in[b * BLOCK : (b + 1) * BLOCK, :]

    def second(ref):
        for w in range(8):
            slot = (half * 8 + w) ^ flip
            ref[slot, spot, 0:D] = grad_out[w * 32 : w * 32 + 16, :]
            ref[slot, spot, D : 2 * D] = grad_out[w * 32 + 16 : w * 32 + 32, :]

    store_split(plan[CORE], keep, send, first, second)


def mlp(call, plan, min_, g, acc, gn, w_in, b_in, w_out):
    rows = g.shape[0]
    tile = lambda k: k + 3 * (k // 3) + 3 * call
    whole = lambda *shape: pl.BlockSpec(shape, lambda k: (0,) * len(shape))
    return pl.pallas_call(
        mlp_kernel,
        grid=(6,),
        out_shape=[
            sds((rows, D), f32),
            sds((rows, D), f32),
            sds((BLOCKS, BLOCK, WIDE_COLS), bf16),
            sds((BLOCKS, BLOCK, WIDE_COLS), bf16),
            sds((1, 6 * TILE), f32),
        ],
        in_specs=[
            SM,
            whole(rows, D),
            whole(rows, D),
            whole(rows, D),
            whole(rows, D),
            pl.BlockSpec((D, TILE), lambda k: (0, tile(k))),
            pl.BlockSpec((1, TILE), lambda k: (0, tile(k))),
            pl.BlockSpec((TILE, D), lambda k: (tile(k), 0)),
        ],
        out_specs=[
            whole(rows, D),
            whole(rows, D),
            whole(BLOCKS, BLOCK, WIDE_COLS),
            whole(BLOCKS, BLOCK, WIDE_COLS),
            pl.BlockSpec((1, TILE), lambda k: (0, k)),
        ],
        scratch_shapes=[pltpu.VMEM((D, rows), bf16)],
        compiler_params=params(56, 1),
        cost_estimate=cost(rows * D * 6 * TILE * 12, 20e6, rows * 6 * TILE * 2),
        name="mlp",
    )(plan, min_, g, acc, gn, w_in, b_in.reshape(1, FF), w_out)


def store_blocks(ref, flip, cols, value):
    for b in range(BLOCKS):
        ref[b ^ flip, :, cols] = value[b * BLOCK : (b + 1) * BLOCK, :]


def cross_back_kernel(
    plan, acc, gn, two, one, g, gain, b_out, w_cross, w_query, w_kv, mix, probs, kv, cq, cin, tokens,
    hid_out, keep, send, gone_out, gimg_out, small_out, gtwo, low, gmix, gcq, gkv,
):
    rows = cq.shape[0]
    images = rows // (2 * SEQ)
    flip = plan[FLIP]
    core = plan[CORE]
    gain1, gain2 = gain[1:2, :].astype(f32), gain[2:3, :].astype(f32)
    bias_out = b_out[...].astype(f32)
    small_out[...] = jnp.zeros_like(small_out)

    def top(i, _):
        span = pl.ds(pl.multiple_of(i * SEQ, SEQ), SEQ)
        x = two[span, :]
        hid_out[i] = (x + (acc[span, :] + bias_out)).astype(bf16)
        up = g[span, :].astype(f32)
        grad = gn[span, :]
        xhat, inv = normed(x)
        small_out[0:1, :] += jnp.sum(grad * xhat, axis=0, keepdims=True)
        small_out[1:2, :] += jnp.sum(grad, axis=0, keepdims=True)
        small_out[4:5, :] += jnp.sum(up, axis=0, keepdims=True)
        total = up + norm_back(grad, xhat, inv, gain2)
        gtwo[span, :] = total
        low[span, :] = total.astype(bf16)
        return 0

    lax.fori_loop(0, rows // SEQ, top, 0)
    gmix[...] = mm_nt(low[...], w_cross[...]).astype(bf16)
    grad_cross = mm_tn(mix[...], low[...]).astype(bf16)
    scaled = lane_masks(SCALE)
    plain = lane_masks(1.0)

    def attend(p, _):
        span = pl.ds(pl.multiple_of(p * 2 * SEQ, 2 * SEQ), 2 * SEQ)
        toks = pl.ds(pl.multiple_of(p * IMG_TOK, IMG_TOK), IMG_TOK)
        for h in range(PAIRS):
            at = 2 * HEAD_DIM * h
            q = two_heads(cq[span, at : at + 128], scaled)
            gm = two_heads(gmix[span, at : at + 128], plain)
            k = kv[toks, at : at + 128]
            v = kv[toks, D + at : D + at + 128]
            pl_ = probs[p, h]
            pf = pl_.astype(f32)
            gp = mm_nt(gm, v)
            delta = jnp.sum(pf * gp, axis=-1, keepdims=True)
            gs = (pf * (gp - delta)).astype(bf16)
            gcq[span, at : at + 128] = (join_heads(mm(gs, k), 2 * SEQ) * SCALE).astype(bf16)
            gkv[toks, at : at + 128] = mm_tn(gs, q).astype(bf16)
            gkv[toks, D + at : D + at + 128] = mm_tn(pl_, gm).astype(bf16)
        return 0

    lax.fori_loop(0, images, attend, 0)
    grad_query = mm_tn(cin[...], gcq[...]).astype(bf16)
    for j in range(2):
        cols = slice(j * D, (j + 1) * D)
        grad_kv = mm_tn(tokens[...], gkv[:, cols]).astype(bf16)

        def first(ref):
            if j == 0:
                store_blocks(ref, flip, slice(0, D), grad_cross)
                store_blocks(ref, flip, slice(D, 2 * D), grad_query)

        def second(ref):
            store_blocks(ref, flip, cols, grad_kv)

        store_split(core, keep, send, first, second)
    gimg_out[...] = mm_nt(gkv[...], w_kv[...])
    gone_out[...] = mm_nt(gcq[...], w_query[...])

    def bottom(i, _):
        span = pl.ds(pl.multiple_of(i * SEQ, SEQ), SEQ)
        grad = gone_out[span, :]
        xhat, inv = normed(one[span, :])
        small_out[2:3, :] += jnp.sum(grad * xhat, axis=0, keepdims=True)
        small_out[3:4, :] += jnp.sum(grad, axis=0, keepdims=True)
        gone_out[span, :] = gtwo[span, :] + norm_back(grad, xhat, inv, gain1)
        return 0

    lax.fori_loop(0, rows // SEQ, bottom, 0)


def cross_back(plan, acc, gn, two, one, g, gain, b_out, w_cross, w_query, w_kv, mix, probs, kv, cq, cin, tokens):
    rows = cq.shape[0]
    toks = tokens.shape[0]
    return pl.pallas_call(
        cross_back_kernel,
        out_shape=[
            sds((rows // SEQ, SEQ, D), bf16),
            sds((BLOCKS, BLOCK, WIDE_COLS), bf16),
            sds((BLOCKS, BLOCK, WIDE_COLS), bf16),
            sds((rows, D), f32),
            sds((toks, D), f32),
            sds((8, D), f32),
        ],
        in_specs=[SM] + [VM] * 16,
        out_specs=[VM] * 6,
        scratch_shapes=[
            pltpu.VMEM((rows, D), f32),
            pltpu.VMEM((rows, D), bf16),
            pltpu.VMEM((rows, D), bf16),
            pltpu.VMEM((rows, D), bf16),
            pltpu.VMEM((toks, 2 * D), bf16),
        ],
        compiler_params=params(),
        cost_estimate=cost(rows * D * D * 20 * 2, 30e6),
        name="cross_back",
    )(plan, acc, gn, two, one, g, gain, b_out.reshape(1, D), w_cross, w_query, w_kv, mix, probs, kv, cq, cin, tokens)


def self_back_kernel(
    plan, gone, x, attn, qkv, probs, mix, gain, w_self, w_qkv,
    hid_out, keep, send, small_out, low, gmix, gqkv, gbase,
):
    rows = x.shape[0]
    flip = plan[FLIP]
    core = plan[CORE]
    gain0 = gain[0:1, :].astype(f32)
    small_out[...] = jnp.zeros_like(small_out)
    low[...] = gone[...].astype(bf16)
    gmix[...] = mm_nt(low[...], w_self[...]).astype(bf16)
    grad_self = mm_tn(mix[...], low[...]).astype(bf16)
    scaled = lane_masks(SCALE)
    plain = lane_masks(1.0)

    def attend(p, _):
        span = pl.ds(pl.multiple_of(p * 2 * SEQ, 2 * SEQ), 2 * SEQ)
        for h in range(PAIRS):
            at = 2 * HEAD_DIM * h
            q = two_heads(qkv[span, at : at + 128], scaled)
            gm = two_heads(gmix[span, at : at + 128], plain)
            k = qkv[span, D + at : D + at + 128]
            v = qkv[span, 2 * D + at : 2 * D + at + 128]
            pl_ = probs[p, h]
            pf = pl_.astype(f32)
            gp = mm_nt(gm, v)
            delta = jnp.sum(pf * gp, axis=-1, keepdims=True)
            gs = (pf * (gp - delta)).astype(bf16)
            gqkv[span, at : at + 128] = (join_heads(mm(gs, k), 2 * SEQ) * SCALE).astype(bf16)
            gqkv[span, D + at : D + at + 128] = mm_tn(gs, q).astype(bf16)
            gqkv[span, 2 * D + at : 2 * D + at + 128] = mm_tn(pl_, gm).astype(bf16)
        return 0

    lax.fori_loop(0, rows // (2 * SEQ), attend, 0)
    for j in range(3):
        grad = mm_tn(attn[...], gqkv[:, j * D : (j + 1) * D]).astype(bf16)

        def first(ref):
            if j == 0:
                store_blocks(ref, flip, slice(0, D), grad_self)
                store_blocks(ref, flip, slice(D, 2 * D), grad)

        def second(ref):
            if j > 0:
                store_blocks(ref, flip, slice((j - 1) * D, j * D), grad)

        store_split(core, keep, send, first, second)
    gbase[...] = mm_nt(gqkv[...], w_qkv[...])

    def bottom(i, _):
        span = pl.ds(pl.multiple_of(i * SEQ, SEQ), SEQ)
        grad = gbase[span, :]
        xhat, inv = normed(x[span, :].astype(f32))
        small_out[0:1, :] += jnp.sum(grad * xhat, axis=0, keepdims=True)
        small_out[1:2, :] += jnp.sum(grad, axis=0, keepdims=True)
        hid_out[i] = gone[span, :] + norm_back(grad, xhat, inv, gain0)
        return 0

    lax.fori_loop(0, rows // SEQ, bottom, 0)


def self_back(plan, gone, x, attn, qkv, probs, mix, gain, w_self, w_qkv):
    rows = x.shape[0]
    return pl.pallas_call(
        self_back_kernel,
        out_shape=[
            sds((rows // SEQ, SEQ, D), f32),
            sds((BLOCKS, BLOCK, WIDE_COLS), bf16),
            sds((BLOCKS, BLOCK, WIDE_COLS), bf16),
            sds((8, D), f32),
        ],
        in_specs=[SM] + [VM] * 9,
        out_specs=[VM] * 4,
        scratch_shapes=[
            pltpu.VMEM((rows, D), bf16),
            pltpu.VMEM((rows, D), bf16),
            pltpu.VMEM((rows, 3 * D), bf16),
            pltpu.VMEM((rows, D), f32),
        ],
        compiler_params=params(),
        cost_estimate=cost(rows * D * D * 16 * 2, 25e6),
        name="self_back",
    )(plan, gone, x, attn, qkv, probs, mix, gain, w_self, w_qkv)


def swap(value, axis, bit):
    size = lax.axis_size(axis)
    return lax.ppermute(value, axis, [(i, i ^ bit) for i in range(size)])


def add(a, b):
    return (a.astype(f32) + b.astype(f32)).astype(bf16)


STEPS = (("narrow", 1), ("wide", 2), ("wide", 4), ("wide", 8))


def reduce_chunk(keep, send):
    got = swap(send, "wide", 1)
    for axis, bit in STEPS:
        half = keep.shape[0] // 2
        out = add(keep[half:], got[half:])
        keep = add(keep[:half], got[:half])
        got = swap(out, axis, bit)
    piece = add(keep, got)
    for axis, bit in STEPS[:0:-1]:
        piece = jnp.concatenate([piece, swap(piece, axis, bit)])
    return piece, swap(piece, "wide", 1)


def load_piece(plan, mine, theirs, half, index, store):
    slot = index ^ (plan[FLIP] % 8)
    core = plan[CORE]

    @pl.when(core == half)
    def _():
        store(mine[slot].astype(f32))

    @pl.when(core != half)
    def _():
        store(theirs[slot].astype(f32))


def finish_columns_kernel(cuts, plan, mine, theirs, *outs):
    for w in range(8):
        for half in range(2):

            def store(value, half=half, w=w):
                for number, src, dst, width in cuts[half]:
                    outs[number][w * BLOCK : (w + 1) * BLOCK, dst : dst + width] = value[:, src : src + width]

            load_piece(plan, mine, theirs, half, w, store)


def finish_columns(plan, pieces, cuts, widths, name):
    return pl.pallas_call(
        functools.partial(finish_columns_kernel, cuts),
        out_shape=[sds((8 * BLOCK, width), f32) for width in widths],
        in_specs=[SM, VM, VM],
        out_specs=[VM] * len(widths),
        compiler_params=params(24),
        cost_estimate=cost(0, 8e6),
        name=name,
    )(plan, *pieces)


def finish_mlp_kernel(plan, mine_a, theirs_a, mine_b, theirs_b, grad_in, grad_out):
    for call, mine, theirs in ((0, mine_a, theirs_a), (1, mine_b, theirs_b)):
        for w in range(8):

            def first(value, w=w, call=call):
                rows = slice(w * BLOCK, (w + 1) * BLOCK)
                for n in range(2):
                    dst = n * 6 * TILE + call * 3 * TILE
                    grad_in[rows, dst : dst + 3 * TILE] = value[:, n * D : (n + 1) * D]

            def second(value, w=w, call=call):
                for j in range(3):
                    for half in range(2):
                        dst = (3 * call + j) * TILE + w * 32 + half * 16
                        grad_out[dst : dst + 16, :] = value[j * 16 : (j + 1) * 16, half * D : (half + 1) * D]

            load_piece(plan, mine, theirs, 0, w, first)
            load_piece(plan, mine, theirs, 1, w, second)


def finish_mlp(plan, a, b):
    return pl.pallas_call(
        finish_mlp_kernel,
        out_shape=[sds((8 * BLOCK, FF), f32), sds((FF // 2, D), f32)],
        in_specs=[SM] + [VM] * 4,
        out_specs=[VM] * 2,
        compiler_params=params(40),
        cost_estimate=cost(0, 16e6),
        name="finish_mlp",
    )(plan, *a, *b)


def plain_sum(value):
    shard = lax.psum_scatter(value, "narrow", scatter_dimension=0, tiled=True)
    return lax.psum(shard, "wide").astype(f32)


def plain_sums(core, chunks):
    whole = []
    for keep, send in chunks:
        first = jnp.where(core == 0, keep, send)
        second = jnp.where(core == 0, send, keep)
        whole.append((first.reshape(D, WIDE_COLS), second))
    grad_in = jnp.stack([whole[0][0].reshape(D, 2, 3 * TILE), whole[1][0].reshape(D, 2, 3 * TILE)], axis=2)
    grad_out = jnp.stack([whole[0][1], whole[1][1]]).reshape(2, 2, 8, 3, 16, 2, D)
    grad_out = grad_out.transpose(1, 0, 3, 2, 5, 4, 6).reshape(FF, D)
    crosses, keys = whole[2][0], whole[2][1].reshape(D, WIDE_COLS)
    front_half, back_half = whole[3][0], whole[3][1].reshape(D, WIDE_COLS)
    return [
        plain_sum(v)
        for v in (
            jnp.concatenate([front_half[:, D:], back_half], axis=1),
            front_half[:, :D],
            crosses[:, D:],
            keys,
            crosses[:, :D],
            grad_in.reshape(D, FF),
            grad_out,
        )
    ]


def local(
    hidden_in, image_tokens, image_group, caption_len, norm_gain, norm_bias, self_qkv, self_out, cross_query,
    cross_kv, cross_out, mlp_in, mlp_bias_in, mlp_out, mlp_bias_out, out_grad,
):
    narrow = lax.axis_size("narrow")
    wide = lax.axis_size("wide")
    images, toks, _ = image_tokens.shape
    mine = images // narrow
    caps = 2 * mine
    rows = caps * SEQ
    n_at, w_at = lax.axis_index("narrow"), lax.axis_index("wide")
    fast = narrow == 2 and wide == 16
    core = w_at % 2
    if fast:
        flip = n_at * 8 + (w_at // 2) % 2 * 4 + (w_at // 4) % 2 * 2 + (w_at // 8) % 2
    else:
        flip = jnp.zeros_like(n_at)
    pos = jnp.stack([n_at, w_at * images, flip, core]).astype(jnp.int32)
    plan = make_plan(narrow, images, image_group, caption_len, pos)
    if narrow == 2:
        own, away = pick_tokens(plan, image_tokens, mine)
        got = swap(away, "narrow", 1)
        tokens = jnp.concatenate([own, got], axis=1).reshape(mine * IMG_TOK, D)
    else:
        every = lax.all_gather(image_tokens, "narrow")
        first = n_at * mine
        tokens = lax.dynamic_slice_in_dim(every, first, mine, 1).transpose(1, 0, 2, 3)
        tokens = tokens.reshape(mine * IMG_TOK, D)
    x, g, attn, qkv, self_probs, self_mix, one, cin, cq = front(
        rows, plan, hidden_in, out_grad, norm_gain, norm_bias, self_qkv, self_out, cross_query
    )
    kv, cross_probs, cross_mix, two, min_ = cross(tokens, cq, one, norm_gain, norm_bias, cross_kv, cross_out)
    zero = jnp.zeros((rows, D), f32)
    acc, gn, keep0, send0, gbias0 = mlp(0, plan, min_, g, zero, zero, mlp_in, mlp_bias_in, mlp_out)
    acc, gn, keep1, send1, gbias1 = mlp(1, plan, min_, g, acc, gn, mlp_in, mlp_bias_in, mlp_out)
    hidden_out, keep2, send2, gone, gimg, small2 = cross_back(
        plan, acc, gn, two, one, g, norm_gain, mlp_bias_out, cross_out, cross_query, cross_kv, cross_mix,
        cross_probs, kv, cq, cin, tokens,
    )
    grad_hidden, keep3, send3, small3 = self_back(
        plan, gone, x, attn, qkv, self_probs, self_mix, norm_gain, self_out, self_qkv
    )
    chunks = ((keep0, send0), (keep1, send1), (keep2, send2), (keep3, send3))
    if fast:
        parts = [reduce_chunk(keep, send) for keep, send in chunks]
        grad_mlp_in, grad_mlp_out = finish_mlp(plan, parts[0], parts[1])
        grad_cross_out, grad_query, grad_kv = finish_columns(
            plan, parts[2], (((0, 0, 0, D), (1, D, 0, D)), ((2, 0, 0, 2 * D),)), (D, D, 2 * D), "finish_cross"
        )
        grad_self_out, grad_qkv = finish_columns(
            plan, parts[3], (((0, 0, 0, D), (1, D, 0, D)), ((1, 0, D, 2 * D),)), (D, 3 * D), "finish_self"
        )
    else:
        grad_qkv, grad_self_out, grad_query, grad_kv, grad_cross_out, grad_mlp_in, grad_mlp_out = plain_sums(
            core, chunks
        )
    bias_in = jnp.stack([gbias0.reshape(2, 3 * TILE), gbias1.reshape(2, 3 * TILE)], axis=1).reshape(4, D)
    small = jnp.concatenate([small3[0:1], small2[2:3], small2[0:1], small3[1:2], small2[3:4], small2[1:2], small2[4:5], bias_in])
    small = lax.psum(small, ("wide", "narrow"))
    share = D // narrow
    columns = lax.dynamic_slice_in_dim(small[:7], n_at * share, share, 1)
    grad_bias_in = lax.dynamic_slice_in_dim(small[7:].reshape(FF), n_at * (FF // narrow), FF // narrow, 0)
    gimg = gimg.reshape(mine, IMG_TOK, D)
    if narrow == 2:
        hid_got = swap(hidden_out.reshape(mine, 2, SEQ, D)[:, 1], "narrow", 1)
        grad_got = swap(grad_hidden.reshape(mine, 2, SEQ, D)[:, 1].astype(bf16), "narrow", 1)
        img_got = swap(gimg[:, toks:].astype(bf16), "narrow", 1)
        final_out = place(OUT_SRC, caps, plan, hidden_out, hid_got, bf16, "place_out")
        final_grad = place(OUT_SRC, caps, plan, grad_hidden, grad_got, f32, "place_grad")
        grad_image = place(IMG_SRC, images, plan, gimg[:, :toks], img_got, f32, "place_image")
    else:
        out_all = lax.all_gather(hidden_out, "narrow", tiled=True)
        grad_all = lax.all_gather(grad_hidden.astype(bf16), "narrow", tiled=True)
        final_out = place(OUT_SRC, caps, plan, out_all, out_all[:1], bf16, "place_out")
        final_grad = place(OUT_SRC, caps, plan, grad_all, grad_all[:1], f32, "place_grad")
        every = lax.all_gather(gimg.astype(bf16), "narrow", tiled=True)
        grad_image = lax.dynamic_slice_in_dim(every, n_at * toks, toks, 1).astype(f32)
    return (
        final_out.reshape(rows, D),
        final_grad.reshape(rows, D),
        grad_image,
        columns[:3],
        columns[3:6],
        grad_qkv,
        grad_self_out,
        grad_query,
        grad_kv,
        grad_cross_out,
        grad_mlp_in,
        grad_bias_in,
        grad_mlp_out,
        columns[6],
    )


def solution(mesh):
    in_specs = (
        P("wide", None),
        P("wide", "narrow", None),
        P("wide"),
        P("wide"),
    ) + (P(),) * 11 + (P("wide", None),)
    out_specs = (
        P(("wide", "narrow"), None),
        P(("wide", "narrow"), None),
        P("wide", "narrow", None),
        P(None, "narrow"),
        P(None, "narrow"),
        P("narrow", None),
        P("narrow", None),
        P("narrow", None),
        P("narrow", None),
        P("narrow", None),
        P("narrow", None),
        P("narrow"),
        P("narrow", None),
        P("narrow"),
    )
    return jax.shard_map(local, mesh=mesh, in_specs=in_specs, out_specs=out_specs, check_vma=False)
```

time: 976 us -> 522 us (0.53)
  matrix products: 232 us -> 0 us
  local copies, waits for them, and re-layouts: 189 us -> 17.5 us
  Pallas kernels: 0 us -> 166 us
  other arithmetic: 118 us -> 12.8 us
  waiting for transfers between devices: 329 us -> 235 us
  starting transfers between devices: 0.96 us -> 34.7 us
  blocking collectives: 81.1 us -> 50.6 us
  between operations: 16.8 us -> 1.39 us
    ppermute x0 -> x40, waiting for transfers between devices: none -> 235 us  [swap(): return lax.ppermute(value, axis, [(i, i ^ bit) for i in range(size)])]
    dot_general x35 -> x0, matrix products: 232 us -> none  [the longest x7 68.1 us: mat_mul(): return jnp.dot(left, right, preferred_element_type=jnp.float32)]
    psum x3 -> x0, waiting for transfers between devices: 206 us -> none  [the longest x1 112 us: local(): lax.psum(shards[5].astype(jnp.bfloat16), 'wide').astype(jnp.float32)]
    pallas_call x0 -> x14, Pallas kernels: none -> 166 us  [the longest x2 36.1 us: mlp(): pl.pallas_call(mlp_kernel, grid=(6,), out_shape=[sds((rows, D), f32), sds...]
    reduce_scatter x6 -> x0, waiting for transfers between devices: 123 us -> none  [the longest x1 62.3 us: local(): lax.psum_scatter(local_grads[9].astype(jnp.bfloat16), 'narrow', scatter_d...]
    unnamed x173 -> x42, local copies, waits for them, and re-layouts: 55.3 us -> 4.66 us
    reshape x8 -> x4, local copies, waits for them, and re-layouts: 52.2 us -> 1.81 us  [the longest x1 0.61 us: local(): small[7:].reshape(FF)]
    convert_element_type x7 -> x1, local copies, waits for them, and re-layouts: 39.3 us -> 0.03 us  [local(): grad_hidden.reshape(mine, 2, SEQ, D)[:, 1].astype(bf16)]
  transfers between devices with their start and end apart: 12 -> 40, of which waited for: 5 -> 25; matrix products, arithmetic and copies ran while one was open for 25% -> 4% of each run, Pallas kernels for 0% -> 23%
where the time goes in v1:
time: 522 us; the launch traced here: 518 us
  waiting for transfers between devices  235 us (45%)
  Pallas kernels  166 us (32%)
  blocking collectives  50.6 us (10%)
  starting transfers between devices  34.7 us (7%)
  local copies, waits for them, and re-layouts  17.5 us (3%)
  other arithmetic  12.8 us (2%)
    ppermute x40, waiting for transfers between devices, swap(): return lax.ppermute(value, axis, [(i, i ^ bit) for i in range(size)])  235 us
    psum x1, blocking collectives, local(): small = lax.psum(small, ('wide', 'narrow'))  50.6 us
    pallas_call x2, Pallas kernels, mlp(): pl.pallas_call(mlp_kernel, grid=(6,), out_shape=[sds((rows, D), f32), sds...  36.1 us
    pallas_call x1, Pallas kernels, cross_back(): pl.pallas_call(cross_back_kernel, out_shape=[sds((rows // SEQ, SEQ, D), b...  35.1 us
    pallas_call x1, Pallas kernels, self_back(): pl.pallas_call(self_back_kernel, out_shape=[sds((rows // SEQ, SEQ, D), f3...  35 us
    ppermute x40, starting transfers between devices, swap(): return lax.ppermute(value, axis, [(i, i ^ bit) for i in range(size)])  34.7 us
    pallas_call x1, Pallas kernels, front(): pl.pallas_call(front_kernel, out_shape=[sds((rows, D), bf16), sds((rows,...  17.7 us
    pallas_call x1, Pallas kernels, cross(): pl.pallas_call(cross_kernel, out_shape=[sds((tokens.shape[0], 2 * D), bf1...  17.1 us
  transfers between devices with their start and end apart: 40, of which 25 were waited for; matrix products, arithmetic and copies ran while one was open for 4% of the time, Pallas kernels for 23%

profile of v1, /device:TPU:0, one launch (start us, length us, event | category | flops | bytes accessed | tf_op | source)
XLA Modules:
  0.0 517.6 jit_solution(1474348674124760187)
XLA Ops:
  2.1 1.4 plan.1
  3.6 1.4 copy-done.1
  5.7 3.0 collective-permute-start
  9.9 17.7 %front.1 = (bf16[512,768]{1,0:T(8,128)(2,1)}, bf16[512,768]{1,0:T(8,128)(2,1)}, bf16[512,768]{1,0:T(8,128)(2,1)}, bf16[512,2304]{1,0:T(8,128)(2,1)}, bf16[4,6,25...) custom-call(s32[48]{0:T(128)} %copy-done.6, ...), custom_call_target="tpu_custom_call" | custom-call | flops 6039797760 | bytes 24000000 | tf_op jit(solution)/shard_map/front/pallas_call | solution.py:284
  27.6 1.2 pad_maximum_fusion
  28.9 17.1 %cross.1 = (bf16[1024,1536]{1,0:T(8,128)(2,1)}, bf16[4,6,256,256]{3,2,1,0:T(8,128)(2,1)}, bf16[512,768]{1,0:T(8,128)(2,1)}, f32[512,768]{1,0:T(8,128)}, bf16[512,768]{1,0:T(8,128)(2,1)}) custom-call(bf16[1024,768]{1,0:T(8,128)(2,1)} %bitcast.22, bf16[512,768]{1,0:T(8,128)(2,1)} %get-tuple-element.59.cq, f32[512,768]{1,0:T(8,128)} %get-tuple-element.60.one, ...), custom_call_target="tpu_custom_call" | custom-call | flops 4831838208 | bytes 20000000 | tf_op jit(solution)/shard_map/cross/pallas_call | solution.py:344
  46.0 1.2 broadcast_in_dim.3.acc_in.gn_in
  47.3 18.1 %mlp.2 = (f32[512,768]{1,0:T(8,128)}, f32[512,768]{1,0:T(8,128)}, bf16[16,48,1536]{2,1,0:T(8,128)(2,1)}, bf16[16,48,1536]{2,1,0:T(8,128)(2,1)}, f32[1,1536]{1,0:T(1,128)}) custom-call(s32[48]{0:T(128)} %copy-done.6, bf16[512,768]{1,0:T(8,128)(2,1)} %get-tuple-element.61.min_ref, bf16[512,768]{1,0:T(8,128)(2,1)} %get-tuple-element.62.g_ref.g, ...), custom_call_target="tpu_custom_call" | custom-call | flops 7247757312 | bytes 20000000 | tf_op jit(solution)/shard_map/mlp/pallas_call | solution.py:418
  65.5 18.0 %mlp.3 = (f32[512,768]{1,0:T(8,128)}, f32[512,768]{1,0:T(8,128)}, bf16[16,48,1536]{2,1,0:T(8,128)(2,1)}, bf16[16,48,1536]{2,1,0:T(8,128)(2,1)}, f32[1,1536]{1,0:T(1,128)}) custom-call(s32[48]{0:T(128)} %copy-done.6, bf16[512,768]{1,0:T(8,128)(2,1)} %get-tuple-element.61.min_ref, bf16[512,768]{1,0:T(8,128)(2,1)} %get-tuple-element.62.g_ref.g, ...), custom_call_target="tpu_custom_call" | custom-call | flops 7247757312 | bytes 20000000 | tf_op jit(solution)/shard_map/mlp/pallas_call | solution.py:418
  83.4 35.1 %cross_back.1 = (bf16[8,64,768]{2,1,0:T(8,128)(2,1)}, bf16[16,48,1536]{2,1,0:T(8,128)(2,1)}, bf16[16,48,1536]{2,1,0:T(8,128)(2,1)}, f32[512,768]{1,0:T(8,128)}, f32[1024,768]{1,0:T(8,128)}, /*index=5*/f32[8,768]{1,0:T(8,128)}) custom-call(s32[48]{0:T(128)} %copy-done.6, f32[512,768]{1,0:T(8,128)} %get-tuple-element.65.acc, f32[512,768]{1,0:T(8,128)} %get-tuple-element.66.gn, ...), custom_call_target="tpu_custom_call" | custom-call | flops 12079595520 | bytes 30000000 | tf_op jit(solution)/shard_map/cross_back/pallas_call | solution.py:542
  118.6 35.0 %self_back.1 = (f32[8,64,768]{2,1,0:T(8,128)}, bf16[16,48,1536]{2,1,0:T(8,128)(2,1)}, bf16[16,48,1536]{2,1,0:T(8,128)(2,1)}, f32[8,768]{1,0:T(8,128)}) custom-call(s32[48]{0:T(128)} %copy-done.6, f32[512,768]{1,0:T(8,128)} %get-tuple-element.73.gone, bf16[512,768]{1,0:T(8,128)(2,1)} %get-tuple-element.74.x, bf16[512,768]{1,0:T(8,128)(2,1)} %get-tuple-element.75.attn, ...), custom_call_target="tpu_custom_call" | custom-call | flops 9663676416 | bytes 25000000 | tf_op jit(solution)/shard_map/self_back/pallas_call | solution.py:630
  155.1 1.6 convert.7
  156.8 1.7 collective-permute-start.2
  159.2 1.8 collective-permute-done.4
  162.1 1.7 collective-permute-start.5
  166.2 34.2 %collective-permute-done.23 = bf16[8,48,1536]{2,1,0:T(8,128)(2,1)S(1)} collective-permute-done((bf16[8,48,1536]{2,1,0:T(8,128)(2,1)S(1)}, bf16[8,48,1536]{2,1,0:T(8,128)(2,1)S(1)}, u32[]{:S(2)}, u32[]{:S(2)}) %collective-permute-start.23) | collective-permute-done | bytes 1179680 | tf_op jit(solution)/shard_map/ppermute | solution.py:654
  201.0 24.6 %collective-permute-done.5 = bf16[8,48,1536]{2,1,0:T(8,128)(2,1)S(1)} collective-permute-done((bf16[8,48,1536]{2,1,0:T(8,128)(2,1)S(1)}, bf16[8,48,1536]{2,1,0:T(8,128)(2,1)S(1)}, u32[]{:S(2)}, u32[]{:S(2)}) %collective-permute-start.5) | collective-permute-done | bytes 1179680 | tf_op jit(solution)/shard_map/ppermute | solution.py:654
  225.6 1.5 collective-permute-start.24
  227.5 23.5 %collective-permute-done.14 = bf16[8,48,1536]{2,1,0:T(8,128)(2,1)S(1)} collective-permute-done((bf16[8,48,1536]{2,1,0:T(8,128)(2,1)S(1)}, bf16[8,48,1536]{2,1,0:T(8,128)(2,1)S(1)}, u32[]{:S(2)}, u32[]{:S(2)}) %collective-permute-start.14) | collective-permute-done | bytes 1179680 | tf_op jit(solution)/shard_map/ppermute | solution.py:654
  250.9 1.5 collective-permute-start.6
  252.8 22.6 %collective-permute-done.32 = bf16[8,48,1536]{2,1,0:T(8,128)(2,1)S(1)} collective-permute-done((bf16[8,48,1536]{2,1,0:T(8,128)(2,1)S(1)}, bf16[8,48,1536]{2,1,0:T(8,128)(2,1)S(1)}, u32[]{:S(2)}, u32[]{:S(2)}) %collective-permute-start.32) | collective-permute-done | bytes 1179680 | tf_op jit(solution)/shard_map/ppermute | solution.py:654
  275.3 1.5 collective-permute-start.15
  277.9 1.6 collective-permute-start.25
  279.7 11.9 %collective-permute-done.15 = bf16[4,48,1536]{2,1,0:T(8,128)(2,1)S(1)} collective-permute-done((bf16[4,48,1536]{2,1,0:T(8,128)(2,1)S(1)}, bf16[4,48,1536]{2,1,0:T(8,128)(2,1)S(1)}, u32[]{:S(2)}, u32[]{:S(2)}) %collective-permute-start.15) | collective-permute-done | bytes 589856 | tf_op jit(solution)/shard_map/ppermute | solution.py:654
  291.6 1.6 collective-permute-start.7
  293.3 9.1 %collective-permute-done.33 = bf16[4,48,1536]{2,1,0:T(8,128)(2,1)S(1)} collective-permute-done((bf16[4,48,1536]{2,1,0:T(8,128)(2,1)S(1)}, bf16[4,48,1536]{2,1,0:T(8,128)(2,1)S(1)}, u32[]{:S(2)}, u32[]{:S(2)}) %collective-permute-start.33) | collective-permute-done | bytes 589856 | tf_op jit(solution)/shard_map/ppermute | solution.py:654
  302.4 1.6 collective-permute-start.16
  304.7 2.7 collective-permute-start.26
  307.5 9.7 %collective-permute-done.16 = bf16[2,48,1536]{2,1,0:T(8,128)(2,1)S(1)} collective-permute-done((bf16[2,48,1536]{2,1,0:T(8,128)(2,1)S(1)}, bf16[2,48,1536]{2,1,0:T(8,128)(2,1)S(1)}, u32[]{:S(2)}, u32[]{:S(2)}) %collective-permute-start.16) | collective-permute-done | bytes 294944 | tf_op jit(solution)/shard_map/ppermute | solution.py:654
  317.1 1.7 collective-permute-start.8
  318.9 1.9 collective-permute-done.34
  320.7 1.7 collective-permute-start.17
  322.5 1.3 collective-permute-start.35
  323.8 11.6 %collective-permute-done.8 = bf16[1,48,1536]{2,1,0:T(8,128)(2,1)S(1)} collective-permute-done((bf16[1,48,1536]{2,1,0:T(8,128)(2,1)S(1)}, bf16[1,48,1536]{2,1,0:T(8,128)(2,1)S(1)}, u32[]{:S(2)}, u32[]{:S(2)}) %collective-permute-start.8) | collective-permute-done | bytes 147488 | tf_op jit(solution)/shard_map/ppermute | solution.py:654
  335.5 9.4 %collective-permute-done.17 = bf16[1,48,1536]{2,1,0:T(8,128)(2,1)S(1)} collective-permute-done((bf16[1,48,1536]{2,1,0:T(8,128)(2,1)S(1)}, bf16[1,48,1536]{2,1,0:T(8,128)(2,1)S(1)}, u32[]{:S(2)}, u32[]{:S(2)}) %collective-permute-start.17) | collective-permute-done | bytes 147488 | tf_op jit(solution)/shard_map/ppermute | solution.py:654
  345.0 7.8 %collective-permute-done.35 = bf16[1,48,1536]{2,1,0:T(8,128)(2,1)S(1)} collective-permute-done((bf16[1,48,1536]{2,1,0:T(8,128)(2,1)S(1)}, bf16[1,48,1536]{2,1,0:T(8,128)(2,1)S(1)}, u32[]{:S(2)}, u32[]{:S(2)}) %collective-permute-start.35) | collective-permute-done | bytes 147488 | tf_op jit(solution)/shard_map/ppermute | solution.py:654
  352.9 3.1 collective-permute-done.27
  356.0 3.2 collective-permute-done.9
  359.2 3.2 collective-permute-done.18
  362.4 1.6 collective-permute-done.36
  364.5 5.7 %collective-permute-done.28 = bf16[2,48,1536]{2,1,0:T(8,128)(2,1)S(1)} collective-permute-done((bf16[2,48,1536]{2,1,0:T(8,128)(2,1)S(1)}, bf16[2,48,1536]{2,1,0:T(8,128)(2,1)S(1)}, u32[]{:S(2)}, u32[]{:S(2)}) %collective-permute-start.28) | collective-permute-done | bytes 294944 | tf_op jit(solution)/shard_map/ppermute | solution.py:654
  370.3 6.3 %collective-permute-done.10 = bf16[2,48,1536]{2,1,0:T(8,128)(2,1)S(1)} collective-permute-done((bf16[2,48,1536]{2,1,0:T(8,128)(2,1)S(1)}, bf16[2,48,1536]{2,1,0:T(8,128)(2,1)S(1)}, u32[]{:S(2)}, u32[]{:S(2)}) %collective-permute-start.10) | collective-permute-done | bytes 294944 | tf_op jit(solution)/shard_map/ppermute | solution.py:654
  376.6 1.5 collective-permute-start.29
  378.2 4.8 collective-permute-done.19
  382.9 1.5 collective-permute-start.11
  384.5 4.7 collective-permute-done.37
  389.1 1.5 collective-permute-start.20
  390.7 2.1 collective-permute-done.29
  392.8 1.5 collective-permute-start.38
  395.5 10.0 %collective-permute-done.11 = bf16[4,48,1536]{2,1,0:T(8,128)(2,1)S(1)} collective-permute-done((bf16[4,48,1536]{2,1,0:T(8,128)(2,1)S(1)}, bf16[4,48,1536]{2,1,0:T(8,128)(2,1)S(1)}, u32[]{:S(2)}, u32[]{:S(2)}) %collective-permute-start.11) | collective-permute-done | bytes 589856 | tf_op jit(solution)/shard_map/ppermute | solution.py:654
  406.6 11.5 %collective-permute-done.20 = bf16[4,48,1536]{2,1,0:T(8,128)(2,1)S(1)} collective-permute-done((bf16[4,48,1536]{2,1,0:T(8,128)(2,1)S(1)}, bf16[4,48,1536]{2,1,0:T(8,128)(2,1)S(1)}, u32[]{:S(2)}, u32[]{:S(2)}) %collective-permute-start.20) | collective-permute-done | bytes 589856 | tf_op jit(solution)/shard_map/ppermute | solution.py:654
  419.2 10.5 %collective-permute-done.38 = bf16[4,48,1536]{2,1,0:T(8,128)(2,1)S(1)} collective-permute-done((bf16[4,48,1536]{2,1,0:T(8,128)(2,1)S(1)}, bf16[4,48,1536]{2,1,0:T(8,128)(2,1)S(1)}, u32[]{:S(2)}, u32[]{:S(2)}) %collective-permute-start.38) | collective-permute-done | bytes 589856 | tf_op jit(solution)/shard_map/ppermute | solution.py:654
  431.4 2.4 slice.451
  436.2 50.6 %psum.7 = f32[11,768]{1,0:T(8,128)S(1)} all-reduce(f32[11,768]{1,0:T(8,128)S(1)} %concatenate.51), channel_id=1, replica_groups=mesh['wide'=16,'narrow'=2] {'wide','narrow'}, use_global_device_ids=true, to_apply=%region_0.1 | all-reduce | flops 8448 | bytes 67584 | tf_op jit(solution)/shard_map/psum | solution.py:833
  487.4 1.5 slice.324.own
  489.5 1.4 dynamic_slice.7
  490.9 1.4 dynamic-slice_reduce_fusion
  492.3 1.5 fusion
  494.9 1.6 place_out.1
  496.5 1.9 place_grad.1
  498.4 3.1 place_image.1
  501.5 4.4 finish_self.1
  505.9 4.4 finish_cross.1
  510.2 7.2 %finish_mlp.1 = (f32[384,3072]{1,0:T(8,128)}, f32[1536,768]{1,0:T(8,128)}) custom-call(s32[48]{0:T(128)S(1)} %copy-done.7, bf16[8,48,1536]{2,1,0:T(8,128)(2,1)} %pad_maximum_fusion.3.mine_a, bf16[8,48,1536]{2,1,0:T(8,128)(2,1)} %collective-permute-done.30.theirs_a, bf16[8,48,1536]{2,1,0:T(8,128)(2,1)} %pad_maximum_fusion.4.mine_b, ...), custom_call_target="tpu_custom_call" | custom-call | bytes 16000000 | tf_op jit(solution)/shard_map/finish_mlp/pallas_call | solution.py:734
  (131 shorter events, 23.4 us)
Async XLA Ops:
  0.8 0.7 copy-start.8
  1.5 0.7 copy-start.9
  3.6 1.4 copy-start.1
  5.0 0.7 copy-start.6
  5.0 3.8 copy-start.18
  5.0 4.3 copy-start.15
  5.7 21.9 %collective-permute-start = (bf16[4,128,768]{2,1,0:T(8,128)(2,1)S(1)}, bf16[4,128,768]{2,1,0:T(8,128)(2,1)S(1)}, u32[]{:S(2)}, u32[]{:S(2)}) collective-permute-start(bf16[4,128,768]{2,1,0:T(8,128)(2,1)S(1)} %get-tuple-element.58), channel_id=1, source_target_pairs={{0,1},{1,0},{2,3},{3,2},{4,5},{5,4},{6,7},{7,6},{8,9},{9,8},{10,11... | collective-permute-start | bytes 2359304 | tf_op jit(solution)/shard_map/ppermute | solution.py:654
  65.4 91.3 %collective-permute-start.22 = (bf16[16,48,1536]{2,1,0:T(8,128)(2,1)}, bf16[16,48,1536]{2,1,0:T(8,128)(2,1)S(1)}, u32[]{:S(2)}, u32[]{:S(2)}) collective-permute-start(bf16[16,48,1536]{2,1,0:T(8,128)(2,1)} %get-tuple-element.95), channel_id=1, source_target_pairs={{0,2},{2,0},{4,6},{6,4},{8,10},{10,8},{12,14},{14,12},{16,18},{18,... | collective-permute-start | bytes 7077896 | tf_op jit(solution)/shard_map/ppermute | solution.py:654
  118.6 35.5 %copy-start.20 = (bf16[16,48,1536]{2,1,0:T(8,128)(2,1)S(1)}, bf16[16,48,1536]{2,1,0:T(8,128)(2,1)}, u32[]{:S(2)}) copy-start(bf16[16,48,1536]{2,1,0:T(8,128)(2,1)} %get-tuple-element.90) | copy-start | bytes 7077892
  118.6 35.6 %copy-start.19 = (bf16[16,48,1536]{2,1,0:T(8,128)(2,1)S(1)}, bf16[16,48,1536]{2,1,0:T(8,128)(2,1)}, u32[]{:S(2)}) copy-start(bf16[16,48,1536]{2,1,0:T(8,128)(2,1)} %get-tuple-element.97) | copy-start | bytes 7077892
  118.6 36.0 %copy-start.2 = (bf16[8,64,768]{2,1,0:T(8,128)(2,1)S(1)}, bf16[8,64,768]{2,1,0:T(8,128)(2,1)}, u32[]{:S(2)}) copy-start(bf16[8,64,768]{2,1,0:T(8,128)(2,1)} %get-tuple-element.72.own) | copy-start | bytes 2359300
  153.6 7.4 %collective-permute-start.4 = (bf16[16,48,1536]{2,1,0:T(8,128)(2,1)}, bf16[16,48,1536]{2,1,0:T(8,128)(2,1)S(1)}, u32[]{:S(2)}, u32[]{:S(2)}) collective-permute-start(bf16[16,48,1536]{2,1,0:T(8,128)(2,1)} %get-tuple-element.86), channel_id=1, source_target_pairs={{0,2},{2,0},{4,6},{6,4},{8,10},{10,8},{12,14},{14,12},{16,18},{18,... | collective-permute-start | bytes 7077896 | tf_op jit(solution)/shard_map/ppermute | solution.py:654
  154.1 8.0 %collective-permute-start.13 = (bf16[16,48,1536]{2,1,0:T(8,128)(2,1)S(1)}, bf16[16,48,1536]{2,1,0:T(8,128)(2,1)S(1)}, u32[]{:S(2)}, u32[]{:S(2)}) collective-permute-start(bf16[16,48,1536]{2,1,0:T(8,128)(2,1)S(1)} %copy-done.20), channel_id=1, source_target_pairs={{0,2},{2,0},{4,6},{6,4},{8,10},{10,8},{12,14},{14,12},{16,18},{18,... | collective-permute-start | bytes 7077896 | tf_op jit(solution)/shard_map/ppermute | solution.py:654
  154.2 10.8 %collective-permute-start.31 = (bf16[16,48,1536]{2,1,0:T(8,128)(2,1)S(1)}, bf16[16,48,1536]{2,1,0:T(8,128)(2,1)S(1)}, u32[]{:S(2)}, u32[]{:S(2)}) collective-permute-start(bf16[16,48,1536]{2,1,0:T(8,128)(2,1)S(1)} %copy-done.19), channel_id=1, source_target_pairs={{0,2},{2,0},{4,6},{6,4},{8,10},{10,8},{12,14},{14,12},{16,18},{18,... | collective-permute-start | bytes 7077896 | tf_op jit(solution)/shard_map/ppermute | solution.py:654
  154.6 276.2 %collective-permute-start.1 = (bf16[4,64,768]{2,1,0:T(8,128)(2,1)S(1)}, bf16[4,64,768]{2,1,0:T(8,128)(2,1)S(1)}, u32[]{:S(2)}, u32[]{:S(2)}) collective-permute-start(bf16[4,64,768]{2,1,0:T(8,128)(2,1)S(1)} %slice_bitcast_fusion.1), channel_id=1, source_target_pairs={{0,1},{1,0},{2,3},{3,2},{4,5},{5,4},{6,7},{7,6},{8,9},{9,8},{10,11... | collective-permute-start | bytes 1179656 | tf_op jit(solution)/shard_map/ppermute | solution.py:654
  155.1 3.4 copy-start.12
  156.8 277.0 %collective-permute-start.2 = (bf16[4,64,768]{2,1,0:T(8,128)(2,1)S(1)}, bf16[4,64,768]{2,1,0:T(8,128)(2,1)S(1)}, u32[]{:S(2)}, u32[]{:S(2)}) collective-permute-start(bf16[4,64,768]{2,1,0:T(8,128)(2,1)S(1)} %slice_bitcast_fusion), channel_id=1, source_target_pairs={{0,1},{1,0},{2,3},{3,2},{4,5},{5,4},{6,7},{7,6},{8,9},{9,8},{10,11... | collective-permute-start | bytes 1179656 | tf_op jit(solution)/shard_map/ppermute | solution.py:654
  158.5 2.9 copy-start.13
  161.0 39.4 %collective-permute-start.23 = (bf16[8,48,1536]{2,1,0:T(8,128)(2,1)S(1)}, bf16[8,48,1536]{2,1,0:T(8,128)(2,1)S(1)}, u32[]{:S(2)}, u32[]{:S(2)}) collective-permute-start(bf16[8,48,1536]{2,1,0:T(8,128)(2,1)S(1)} %get-tuple-element.103), channel_id=1, source_target_pairs={{0,1},{1,0},{2,3},{3,2},{4,5},{5,4},{6,7},{7,6},{8,9},{9,8},{10,11... | collective-permute-start | bytes 3538952 | tf_op jit(solution)/shard_map/ppermute | solution.py:654
  161.4 2.5 copy-start.11
  162.1 63.5 %collective-permute-start.5 = (bf16[8,48,1536]{2,1,0:T(8,128)(2,1)S(1)}, bf16[8,48,1536]{2,1,0:T(8,128)(2,1)S(1)}, u32[]{:S(2)}, u32[]{:S(2)}) collective-permute-start(bf16[8,48,1536]{2,1,0:T(8,128)(2,1)S(1)} %get-tuple-element.107), channel_id=1, source_target_pairs={{0,1},{1,0},{2,3},{3,2},{4,5},{5,4},{6,7},{7,6},{8,9},{9,8},{10,11... | collective-permute-start | bytes 3538952 | tf_op jit(solution)/shard_map/ppermute | solution.py:654
  163.8 1.7 copy-start.10
  165.0 85.9 %collective-permute-start.14 = (bf16[8,48,1536]{2,1,0:T(8,128)(2,1)S(1)}, bf16[8,48,1536]{2,1,0:T(8,128)(2,1)S(1)}, u32[]{:S(2)}, u32[]{:S(2)}) collective-permute-start(bf16[8,48,1536]{2,1,0:T(8,128)(2,1)S(1)} %get-tuple-element.105), channel_id=1, source_target_pairs={{0,1},{1,0},{2,3},{3,2},{4,5},{5,4},{6,7},{7,6},{8,9},{9,8},{10,11... | collective-permute-start | bytes 3538952 | tf_op jit(solution)/shard_map/ppermute | solution.py:654
  200.4 75.0 %collective-permute-start.32 = (bf16[8,48,1536]{2,1,0:T(8,128)(2,1)S(1)}, bf16[8,48,1536]{2,1,0:T(8,128)(2,1)S(1)}, u32[]{:S(2)}, u32[]{:S(2)}) collective-permute-start(bf16[8,48,1536]{2,1,0:T(8,128)(2,1)S(1)} %get-tuple-element.101), channel_id=1, source_target_pairs={{0,1},{1,0},{2,3},{3,2},{4,5},{5,4},{6,7},{7,6},{8,9},{9,8},{10,11... | collective-permute-start | bytes 3538952 | tf_op jit(solution)/shard_map/ppermute | solution.py:654
  225.6 51.5 %collective-permute-start.24 = (bf16[4,48,1536]{2,1,0:T(8,128)(2,1)S(1)}, bf16[4,48,1536]{2,1,0:T(8,128)(2,1)S(1)}, u32[]{:S(2)}, u32[]{:S(2)}) collective-permute-start(bf16[4,48,1536]{2,1,0:T(8,128)(2,1)S(1)} %get-tuple-element.111), channel_id=1, source_target_pairs={{0,4},{2,6},{4,0},{6,2},{8,12},{10,14},{12,8},{14,10},{16,20},{18,... | collective-permute-start | bytes 1769480 | tf_op jit(solution)/shard_map/ppermute | solution.py:654
  250.9 27.0 %collective-permute-start.6 = (bf16[4,48,1536]{2,1,0:T(8,128)(2,1)S(1)}, bf16[4,48,1536]{2,1,0:T(8,128)(2,1)S(1)}, u32[]{:S(2)}, u32[]{:S(2)}) collective-permute-start(bf16[4,48,1536]{2,1,0:T(8,128)(2,1)S(1)} %get-tuple-element.115), channel_id=1, source_target_pairs={{0,4},{2,6},{4,0},{6,2},{8,12},{10,14},{12,8},{14,10},{16,20},{18,... | collective-permute-start | bytes 1769480 | tf_op jit(solution)/shard_map/ppermute | solution.py:654
  275.3 16.3 %collective-permute-start.15 = (bf16[4,48,1536]{2,1,0:T(8,128)(2,1)S(1)}, bf16[4,48,1536]{2,1,0:T(8,128)(2,1)S(1)}, u32[]{:S(2)}, u32[]{:S(2)}) collective-permute-start(bf16[4,48,1536]{2,1,0:T(8,128)(2,1)S(1)} %get-tuple-element.113), channel_id=1, source_target_pairs={{0,4},{2,6},{4,0},{6,2},{8,12},{10,14},{12,8},{14,10},{16,20},{18,... | collective-permute-start | bytes 1769480 | tf_op jit(solution)/shard_map/ppermute | solution.py:654
  277.2 25.3 %collective-permute-start.33 = (bf16[4,48,1536]{2,1,0:T(8,128)(2,1)S(1)}, bf16[4,48,1536]{2,1,0:T(8,128)(2,1)S(1)}, u32[]{:S(2)}, u32[]{:S(2)}) collective-permute-start(bf16[4,48,1536]{2,1,0:T(8,128)(2,1)S(1)} %get-tuple-element.109), channel_id=1, source_target_pairs={{0,4},{2,6},{4,0},{6,2},{8,12},{10,14},{12,8},{14,10},{16,20},{18,... | collective-permute-start | bytes 1769480 | tf_op jit(solution)/shard_map/ppermute | solution.py:654
  277.9 26.3 %collective-permute-start.25 = (bf16[2,48,1536]{2,1,0:T(8,128)(2,1)S(1)}, bf16[2,48,1536]{2,1,0:T(8,128)(2,1)S(1)}, u32[]{:S(2)}, u32[]{:S(2)}) collective-permute-start(bf16[2,48,1536]{2,1,0:T(8,128)(2,1)S(1)} %get-tuple-element.119), channel_id=1, source_target_pairs={{0,8},{2,10},{4,12},{6,14},{8,0},{10,2},{12,4},{14,6},{16,24},{18,... | collective-permute-start | bytes 884744 | tf_op jit(solution)/shard_map/ppermute | solution.py:654
  291.6 13.1 %collective-permute-start.7 = (bf16[2,48,1536]{2,1,0:T(8,128)(2,1)S(1)}, bf16[2,48,1536]{2,1,0:T(8,128)(2,1)S(1)}, u32[]{:S(2)}, u32[]{:S(2)}) collective-permute-start(bf16[2,48,1536]{2,1,0:T(8,128)(2,1)S(1)} %get-tuple-element.123), channel_id=1, source_target_pairs={{0,8},{2,10},{4,12},{6,14},{8,0},{10,2},{12,4},{14,6},{16,24},{18,... | collective-permute-start | bytes 884744 | tf_op jit(solution)/shard_map/ppermute | solution.py:654
  302.4 14.7 %collective-permute-start.16 = (bf16[2,48,1536]{2,1,0:T(8,128)(2,1)S(1)}, bf16[2,48,1536]{2,1,0:T(8,128)(2,1)S(1)}, u32[]{:S(2)}, u32[]{:S(2)}) collective-permute-start(bf16[2,48,1536]{2,1,0:T(8,128)(2,1)S(1)} %get-tuple-element.121), channel_id=1, source_target_pairs={{0,8},{2,10},{4,12},{6,14},{8,0},{10,2},{12,4},{14,6},{16,24},{18,... | collective-permute-start | bytes 884744 | tf_op jit(solution)/shard_map/ppermute | solution.py:654
  304.2 16.6 %collective-permute-start.34 = (bf16[2,48,1536]{2,1,0:T(8,128)(2,1)S(1)}, bf16[2,48,1536]{2,1,0:T(8,128)(2,1)S(1)}, u32[]{:S(2)}, u32[]{:S(2)}) collective-permute-start(bf16[2,48,1536]{2,1,0:T(8,128)(2,1)S(1)} %get-tuple-element.117), channel_id=1, source_target_pairs={{0,8},{2,10},{4,12},{6,14},{8,0},{10,2},{12,4},{14,6},{16,24},{18,... | collective-permute-start | bytes 884744 | tf_op jit(solution)/shard_map/ppermute | solution.py:654
  304.7 17.7 %collective-permute-start.26 = (bf16[1,48,1536]{2,1,0:T(8,128)(2,1)S(1)}, bf16[1,48,1536]{2,1,0:T(8,128)(2,1)S(1)}, u32[]{:S(2)}, u32[]{:S(2)}) collective-permute-start(bf16[1,48,1536]{2,1,0:T(8,128)(2,1)S(1)} %add_convert_fusion.28), channel_id=1, source_target_pairs={{0,16},{2,18},{4,20},{6,22},{8,24},{10,26},{12,28},{14,30},{16,0},... | collective-permute-start | bytes 442376 | tf_op jit(solution)/shard_map/ppermute | solution.py:654
  317.1 18.3 %collective-permute-start.8 = (bf16[1,48,1536]{2,1,0:T(8,128)(2,1)S(1)}, bf16[1,48,1536]{2,1,0:T(8,128)(2,1)S(1)}, u32[]{:S(2)}, u32[]{:S(2)}) collective-permute-start(bf16[1,48,1536]{2,1,0:T(8,128)(2,1)S(1)} %add_convert_fusion.34), channel_id=1, source_target_pairs={{0,16},{2,18},{4,20},{6,22},{8,24},{10,26},{12,28},{14,30},{16,0},... | collective-permute-start | bytes 442376 | tf_op jit(solution)/shard_map/ppermute | solution.py:654
  320.7 24.2 %collective-permute-start.17 = (bf16[1,48,1536]{2,1,0:T(8,128)(2,1)S(1)}, bf16[1,48,1536]{2,1,0:T(8,128)(2,1)S(1)}, u32[]{:S(2)}, u32[]{:S(2)}) collective-permute-start(bf16[1,48,1536]{2,1,0:T(8,128)(2,1)S(1)} %add_convert_fusion.31), channel_id=1, source_target_pairs={{0,16},{2,18},{4,20},{6,22},{8,24},{10,26},{12,28},{14,30},{16,0},... | collective-permute-start | bytes 442376 | tf_op jit(solution)/shard_map/ppermute | solution.py:654
  322.5 30.3 %collective-permute-start.35 = (bf16[1,48,1536]{2,1,0:T(8,128)(2,1)S(1)}, bf16[1,48,1536]{2,1,0:T(8,128)(2,1)S(1)}, u32[]{:S(2)}, u32[]{:S(2)}) collective-permute-start(bf16[1,48,1536]{2,1,0:T(8,128)(2,1)S(1)} %add_convert_fusion.25), channel_id=1, source_target_pairs={{0,16},{2,18},{4,20},{6,22},{8,24},{10,26},{12,28},{14,30},{16,0},... | collective-permute-start | bytes 442376 | tf_op jit(solution)/shard_map/ppermute | solution.py:654
  335.4 20.5 %collective-permute-start.27 = (bf16[1,48,1536]{2,1,0:T(8,128)(2,1)S(1)}, bf16[1,48,1536]{2,1,0:T(8,128)(2,1)S(1)}, u32[]{:S(2)}, u32[]{:S(2)}) collective-permute-start(bf16[1,48,1536]{2,1,0:T(8,128)(2,1)S(1)} %add_convert_fusion.27), channel_id=1, source_target_pairs={{0,16},{2,18},{4,20},{6,22},{8,24},{10,26},{12,28},{14,30},{16,0},... | collective-permute-start | bytes 442376 | tf_op jit(solution)/shard_map/ppermute | solution.py:654
  344.9 14.3 %collective-permute-start.9 = (bf16[1,48,1536]{2,1,0:T(8,128)(2,1)S(1)}, bf16[1,48,1536]{2,1,0:T(8,128)(2,1)S(1)}, u32[]{:S(2)}, u32[]{:S(2)}) collective-permute-start(bf16[1,48,1536]{2,1,0:T(8,128)(2,1)S(1)} %add_convert_fusion.33), channel_id=1, source_target_pairs={{0,16},{2,18},{4,20},{6,22},{8,24},{10,26},{12,28},{14,30},{16,0},... | collective-permute-start | bytes 442376 | tf_op jit(solution)/shard_map/ppermute | solution.py:654
  352.8 9.6 %collective-permute-start.18 = (bf16[1,48,1536]{2,1,0:T(8,128)(2,1)S(1)}, bf16[1,48,1536]{2,1,0:T(8,128)(2,1)S(1)}, u32[]{:S(2)}, u32[]{:S(2)}) collective-permute-start(bf16[1,48,1536]{2,1,0:T(8,128)(2,1)S(1)} %add_convert_fusion.30), channel_id=1, source_target_pairs={{0,16},{2,18},{4,20},{6,22},{8,24},{10,26},{12,28},{14,30},{16,0},... | collective-permute-start | bytes 442376 | tf_op jit(solution)/shard_map/ppermute | solution.py:654
  356.0 8.0 %collective-permute-start.36 = (bf16[1,48,1536]{2,1,0:T(8,128)(2,1)S(1)}, bf16[1,48,1536]{2,1,0:T(8,128)(2,1)S(1)}, u32[]{:S(2)}, u32[]{:S(2)}) collective-permute-start(bf16[1,48,1536]{2,1,0:T(8,128)(2,1)S(1)} %add_convert_fusion.24), channel_id=1, source_target_pairs={{0,16},{2,18},{4,20},{6,22},{8,24},{10,26},{12,28},{14,30},{16,0},... | collective-permute-start | bytes 442376 | tf_op jit(solution)/shard_map/ppermute | solution.py:654
  359.2 11.1 %collective-permute-start.28 = (bf16[2,48,1536]{2,1,0:T(8,128)(2,1)S(1)}, bf16[2,48,1536]{2,1,0:T(8,128)(2,1)S(1)}, u32[]{:S(2)}, u32[]{:S(2)}) collective-permute-start(bf16[2,48,1536]{2,1,0:T(8,128)(2,1)S(1)} %pad_maximum_fusion.11), channel_id=1, source_target_pairs={{0,8},{2,10},{4,12},{6,14},{8,0},{10,2},{12,4},{14,6},{16,24},{18,... | collective-permute-start | bytes 884744 | tf_op jit(solution)/shard_map/ppermute | solution.py:654
  362.4 14.2 %collective-permute-start.10 = (bf16[2,48,1536]{2,1,0:T(8,128)(2,1)S(1)}, bf16[2,48,1536]{2,1,0:T(8,128)(2,1)S(1)}, u32[]{:S(2)}, u32[]{:S(2)}) collective-permute-start(bf16[2,48,1536]{2,1,0:T(8,128)(2,1)S(1)} %pad_maximum_fusion.9), channel_id=1, source_target_pairs={{0,8},{2,10},{4,12},{6,14},{8,0},{10,2},{12,4},{14,6},{16,24},{18,... | collective-permute-start | bytes 884744 | tf_op jit(solution)/shard_map/ppermute | solution.py:654
  364.0 18.9 %collective-permute-start.19 = (bf16[2,48,1536]{2,1,0:T(8,128)(2,1)S(1)}, bf16[2,48,1536]{2,1,0:T(8,128)(2,1)S(1)}, u32[]{:S(2)}, u32[]{:S(2)}) collective-permute-start(bf16[2,48,1536]{2,1,0:T(8,128)(2,1)S(1)} %pad_maximum_fusion.10), channel_id=1, source_target_pairs={{0,8},{2,10},{4,12},{6,14},{8,0},{10,2},{12,4},{14,6},{16,24},{18,... | collective-permute-start | bytes 884744 | tf_op jit(solution)/shard_map/ppermute | solution.py:654
  370.3 18.9 %collective-permute-start.37 = (bf16[2,48,1536]{2,1,0:T(8,128)(2,1)S(1)}, bf16[2,48,1536]{2,1,0:T(8,128)(2,1)S(1)}, u32[]{:S(2)}, u32[]{:S(2)}) collective-permute-start(bf16[2,48,1536]{2,1,0:T(8,128)(2,1)S(1)} %pad_maximum_fusion.12), channel_id=1, source_target_pairs={{0,8},{2,10},{4,12},{6,14},{8,0},{10,2},{12,4},{14,6},{16,24},{18,... | collective-permute-start | bytes 884744 | tf_op jit(solution)/shard_map/ppermute | solution.py:654
  376.6 16.2 %collective-permute-start.29 = (bf16[4,48,1536]{2,1,0:T(8,128)(2,1)S(1)}, bf16[4,48,1536]{2,1,0:T(8,128)(2,1)S(1)}, u32[]{:S(2)}, u32[]{:S(2)}) collective-permute-start(bf16[4,48,1536]{2,1,0:T(8,128)(2,1)S(1)} %pad_maximum_fusion.7), channel_id=1, source_target_pairs={{0,4},{2,6},{4,0},{6,2},{8,12},{10,14},{12,8},{14,10},{16,20},{18,... | collective-permute-start | bytes 1769480 | tf_op jit(solution)/shard_map/ppermute | solution.py:654
  382.9 22.5 %collective-permute-start.11 = (bf16[4,48,1536]{2,1,0:T(8,128)(2,1)S(1)}, bf16[4,48,1536]{2,1,0:T(8,128)(2,1)S(1)}, u32[]{:S(2)}, u32[]{:S(2)}) collective-permute-start(bf16[4,48,1536]{2,1,0:T(8,128)(2,1)S(1)} %pad_maximum_fusion.5), channel_id=1, source_target_pairs={{0,4},{2,6},{4,0},{6,2},{8,12},{10,14},{12,8},{14,10},{16,20},{18,... | collective-permute-start | bytes 1769480 | tf_op jit(solution)/shard_map/ppermute | solution.py:654
  389.1 28.9 %collective-permute-start.20 = (bf16[4,48,1536]{2,1,0:T(8,128)(2,1)S(1)}, bf16[4,48,1536]{2,1,0:T(8,128)(2,1)S(1)}, u32[]{:S(2)}, u32[]{:S(2)}) collective-permute-start(bf16[4,48,1536]{2,1,0:T(8,128)(2,1)S(1)} %pad_maximum_fusion.6), channel_id=1, source_target_pairs={{0,4},{2,6},{4,0},{6,2},{8,12},{10,14},{12,8},{14,10},{16,20},{18,... | collective-permute-start | bytes 1769480 | tf_op jit(solution)/shard_map/ppermute | solution.py:654
  392.8 36.9 %collective-permute-start.38 = (bf16[4,48,1536]{2,1,0:T(8,128)(2,1)S(1)}, bf16[4,48,1536]{2,1,0:T(8,128)(2,1)S(1)}, u32[]{:S(2)}, u32[]{:S(2)}) collective-permute-start(bf16[4,48,1536]{2,1,0:T(8,128)(2,1)S(1)} %pad_maximum_fusion.8), channel_id=1, source_target_pairs={{0,4},{2,6},{4,0},{6,2},{8,12},{10,14},{12,8},{14,10},{16,20},{18,... | collective-permute-start | bytes 1769480 | tf_op jit(solution)/shard_map/ppermute | solution.py:654
  405.4 104.8 %collective-permute-start.30 = (bf16[8,48,1536]{2,1,0:T(8,128)(2,1)}, bf16[8,48,1536]{2,1,0:T(8,128)(2,1)}, u32[]{:S(2)}, u32[]{:S(2)}) collective-permute-start(bf16[8,48,1536]{2,1,0:T(8,128)(2,1)} %pad_maximum_fusion.3.mine_a), channel_id=1, source_target_pairs={{0,2},{2,0},{4,6},{6,4},{8,10},{10,8},{12,14},{14,12},{16,18},{18,... | collective-permute-start | bytes 3538952 | tf_op jit(solution)/shard_map/ppermute | solution.py:654
  418.1 83.4 %collective-permute-start.12 = (bf16[8,48,1536]{2,1,0:T(8,128)(2,1)}, bf16[8,48,1536]{2,1,0:T(8,128)(2,1)}, u32[]{:S(2)}, u32[]{:S(2)}) collective-permute-start(bf16[8,48,1536]{2,1,0:T(8,128)(2,1)} %pad_maximum_fusion.1.mine), channel_id=1, source_target_pairs={{0,2},{2,0},{4,6},{6,4},{8,10},{10,8},{12,14},{14,12},{16,18},{18,... | collective-permute-start | bytes 3538952 | tf_op jit(solution)/shard_map/ppermute | solution.py:654
  429.7 76.2 %collective-permute-start.21 = (bf16[8,48,1536]{2,1,0:T(8,128)(2,1)}, bf16[8,48,1536]{2,1,0:T(8,128)(2,1)}, u32[]{:S(2)}, u32[]{:S(2)}) collective-permute-start(bf16[8,48,1536]{2,1,0:T(8,128)(2,1)} %pad_maximum_fusion.2.mine), channel_id=1, source_target_pairs={{0,2},{2,0},{4,6},{6,4},{8,10},{10,8},{12,14},{14,12},{16,18},{18,... | collective-permute-start | bytes 3538952 | tf_op jit(solution)/shard_map/ppermute | solution.py:654
  430.8 4.2 copy-start.16
  430.8 4.3 copy-start.17
  430.8 5.2 %copy-start.14 = (f32[8,768]{1,0:T(8,128)S(1)}, f32[8,768]{1,0:T(8,128)}, u32[]{:S(2)}) copy-start(f32[8,768]{1,0:T(8,128)} %get-tuple-element.82) | copy-start | bytes 73732
  430.8 79.4 %collective-permute-start.39 = (bf16[8,48,1536]{2,1,0:T(8,128)(2,1)}, bf16[8,48,1536]{2,1,0:T(8,128)(2,1)}, u32[]{:S(2)}, u32[]{:S(2)}) collective-permute-start(bf16[8,48,1536]{2,1,0:T(8,128)(2,1)} %pad_maximum_fusion.4.mine_b), channel_id=1, source_target_pairs={{0,2},{2,0},{4,6},{6,4},{8,10},{10,8},{12,14},{14,12},{16,18},{18,... | collective-permute-start | bytes 3538952 | tf_op jit(solution)/shard_map/ppermute | solution.py:654
  433.8 0.7 copy-start.4
  434.5 63.9 %collective-permute-start.3 = (bf16[4,128,768]{2,1,0:T(8,128)(2,1)}, bf16[4,128,768]{2,1,0:T(8,128)(2,1)}, u32[]{:S(2)}, u32[]{:S(2)}) collective-permute-start(bf16[4,128,768]{2,1,0:T(8,128)(2,1)} %slice.451), channel_id=1, source_target_pairs={{0,1},{1,0},{2,3},{3,2},{4,5},{5,4},{6,7},{7,6},{8,9},{9,8},{10,11... | collective-permute-start | bytes 2359304 | tf_op jit(solution)/shard_map/ppermute | solution.py:654
  487.4 6.4 %copy-start.7 = (s32[48]{0:T(128)S(1)}, s32[48]{0:T(128)}, u32[]{:S(2)}) copy-start(s32[48]{0:T(128)} %copy-done.6) | copy-start | bytes 580
  488.9 7.5 %copy-start = (f32[8,64,768]{2,1,0:T(8,128)S(1)}, f32[8,64,768]{2,1,0:T(8,128)}, u32[]{:S(2)}) copy-start(f32[8,64,768]{2,1,0:T(8,128)} %get-tuple-element.79.own) | copy-start | bytes 4718596
  493.8 1.1 copy-start.3
  494.9 1.6 copy-start.5
